TPU v7x, 1024 devices: a whole 8x8x8 slice. The times are simulated.
1024 devices in a mesh: rep: 8 (over x_hi, core), shard: 128 (over z, x_lo, y).
Axes of the slice: x: 8 (x_hi: 4, x_lo: 2; x = x_hi * 2 + x_lo), y: 8, z: 8, core: 2. Of those that a mesh axis runs over, the one named last changes fastest.
Arguments:
- latents: bfloat16 [1024, 24, 20, 384], P(('rep', 'shard')), may hold values from -6 to 6
- norm_gain: float32 [384], replicated, may hold values from 0.1 to 1.9
- norm_bias: float32 [384], replicated, may hold values from -3 to 3
- conv_weight: bfloat16 [3, 1152, 384], P(None, 'shard'), may hold values from -0.109375 to 0.109375
- cotangent: bfloat16 [1024, 24, 20, 384], P(('rep', 'shard')), may hold values from -6 to 6
Outputs:
- output: bfloat16 [1024, 24, 20, 384], P(('rep', 'shard'))
- grad_input: bfloat16 [1024, 24, 20, 384], P(('rep', 'shard'))
- grad_weight: float32 [3, 1152, 384], P(None, 'shard')
All inputs are finite; a program needn't handle non-finite values.
Results may differ from a plain program's by a relative error of at most 0.0035.
Values may be sent and summed in bfloat16 or wider, within the bound.
No kernel may reach another device: no remote copies, remote signals or barrier semaphores. Data moves between devices by JAX's collectives and lax.ppermute only.
A program may use at most 128 MiB of HBM per device.

v0:
```python
import jax
import jax.numpy as jnp
from jax import lax
from jax.sharding import PartitionSpec as P

GROUPS = 32


def norm_act(values, norm_gain, norm_bias):
    shape = values.shape
    per = shape[-1] // GROUPS
    grouped = values.reshape(shape[:-1] + (GROUPS, per))
    mean = jnp.mean(grouped, axis=(1, 2, 4), keepdims=True)
    centred = grouped - mean
    variance = jnp.mean(centred * centred, axis=(1, 2, 4), keepdims=True)
    normed = (centred / jnp.sqrt(variance + 1e-05)).reshape(shape) * norm_gain + norm_bias
    return jax.nn.silu(normed)


def body(latents, norm_gain, norm_bias, conv_weight, cotangent):
    count, rows, cols, chans = latents.shape
    shard_count = lax.axis_size("shard")
    rep_count = lax.axis_size("rep")
    scale = 1.0 / (count * shard_count * rep_count)
    cells = count * rows * cols
    weight_full = lax.all_gather(conv_weight, "shard", axis=1, tiled=True)
    values = latents.astype(jnp.float32)
    activated = norm_act(values, norm_gain, norm_bias).astype(jnp.bfloat16)
    padded = jnp.pad(activated, ((0, 0), (1, 1), (1, 1), (0, 0)))
    flat_up = cotangent.reshape(cells, chans)
    pre = jnp.zeros((cells, chans), jnp.float32)
    total = jnp.zeros((count, rows + 2, cols + 2, chans), jnp.float32)
    patch_rows = []
    for i in range(3):
        taps = [padded[:, i : i + rows, j : j + cols, :] for j in range(3)]
        patches = jnp.concatenate(taps, axis=-1).reshape(cells, 3 * chans)
        patch_rows.append(patches)
        pre = pre + jnp.dot(patches, weight_full[i], preferred_element_type=jnp.float32)
        patch_grad = jnp.einsum(
            "pc,kc->pk", flat_up, weight_full[i], preferred_element_type=jnp.float32
        )
        parts = patch_grad.reshape(count, rows, cols, 3, chans)
        for j in range(3):
            total = total + jnp.pad(parts[:, :, :, j, :], ((0, 0), (i, 2 - i), (j, 2 - j), (0, 0)))
    output = (values + pre.reshape(values.shape)).astype(jnp.bfloat16)
    act_grad = total[:, 1:-1, 1:-1, :]
    unused, pullback = jax.vjp(lambda v: norm_act(v, norm_gain, norm_bias), values)
    back = pullback(act_grad)[0]
    grad_input = (cotangent.astype(jnp.float32) + back).astype(jnp.bfloat16)
    blocks = []
    for i in range(3):
        window = patch_rows[i]
        blocks.append(
            lax.psum_scatter(
                jnp.einsum("pk,pc->kc", window, flat_up, preferred_element_type=jnp.float32)
                * scale,
                "shard",
                scatter_dimension=0,
                tiled=True,
            )
        )
    grad_weight = lax.psum(jnp.stack(blocks), "rep")
    return (output, grad_input, grad_weight)


def solution(mesh):
    placed = (
        P(("rep", "shard"), None, None, None),
        P(),
        P(),
        P(None, "shard", None),
        P(("rep", "shard"), None, None, None),
    )
    return jax.shard_map(
        body,
        mesh=mesh,
        in_specs=placed,
        out_specs=(
            P(("rep", "shard"), None, None, None),
            P(("rep", "shard"), None, None, None),
            P(None, "shard", None),
        ),
        check_vma=False,
    )
```

profile of v0, /device:TPU:1, one launch (start us, length us, event | category | flops | bytes accessed | tf_op | source)
XLA Modules:
  0.0 1861.8 jit_solution(3564845355227594370)
XLA Ops:
  7.9 1.1 convert_reduce_fusion
  9.4 1.1 fusion.22
  11.2 520.2 %all-gather.2.cloned.1.call-done = bf16[3,1152,384]{2,0,1:T(4,128)(2,1)} async-done(((bf16[3,9,384]{2,0,1:T(4,128)(2,1)}), bf16[3,1152,384]{2,0,1:T(4,128)(2,1)}) %all-gather.2.cloned.1.call-update) | async-done | bytes 2654224 | tf_op jit(solution)/shard_map/all_gather | solution.py:26
  531.4 8.8 fusion.41
  546.4 0.9 fusion.25
  547.7 2.1 fusion.1
  549.8 2.1 fusion
  551.9 2.1 fusion.2
  554.0 1.3 dynamic-slice
  555.9 1.0 copy.30
  557.8 1.8 copy.28
  560.7 1.3 pad_maximum_fusion
  562.0 1.2 copy.26
  563.2 2.2 reshape.182
  566.3 1.9 concatenate.20
  568.2 1.8 concatenate.19
  570.1 1.2 copy.32
  571.3 1.4 reshape.183
  572.8 2.4 fusion.20
  576.0 1.6 convolution_add_fusion
  577.6 1.2 reshape.184
  578.8 1.2 add_convert_fusion
  580.0 1169.3 %all-reduce.16.cloned.1.call-done = (f32[1152,384]{1,0:T(8,128)}, f32[1152,384]{1,0:T(8,128)}, f32[1152,384]{1,0:T(8,128)}) async-done(((f32[1152,384]{1,0:T(8,128)}, f32[1152,384]{1,0:T(8,128)}, f32[1152,384]{1,0:T(8,128)}), (f32[1152,384]{1,0:T(8,128)}, f32[1152,384]{1,0:T(8,128)}, f32[1152,384]{1,0:T(8,128)})) %all-reduce.16.cloned.1.call-update) | async-done | bytes 5308432
  1751.6 102.8 %psum.7 = f32[3,9,384]{2,1,0:T(8,128)S(1)} all-reduce(f32[3,9,384]{2,1,0:T(8,128)S(1)} %pad_maximum_fusion.2), channel_id=1, replica_groups=mesh['rep'=8,'shard'=128] {'rep'}, use_global_device_ids=true, to_apply=%region_11.12 | all-reduce | flops 10368 | bytes 82944 | tf_op jit(solution)/shard_map/psum | solution.py:62
  (84 shorter events, 14.7 us)
Async XLA Ops:
  7.2 524.2 %all-gather.2.cloned.1.call-start = ((), (), s32[]{:S(2)}) async-start(), calls=%async_computation | async-start | bytes 3566592 | tf_op jit(solution)/shard_map/all_gather | solution.py:26
  7.9 1741.4 %all-reduce.16.cloned.1.call-start = ((), (), s32[]{:S(2)}) async-start(), calls=%async_computation.1 | async-start | bytes 10616832
  540.4 1.0 copy-start.1
  540.5 2.5 copy-start.2
  543.2 0.9 copy-start.4
  545.4 1.0 copy-start
  545.4 1.0 copy-start.17
  545.4 1.0 copy-start.18
  547.6 2.2 copy-start.12
  547.7 2.2 copy-start.13
  547.7 2.2 copy-start.5
  547.7 2.2 copy-start.7
  547.7 4.2 copy-start.9
  547.7 4.2 copy-start.10
  547.7 4.2 copy-start.11
  565.5 4.5 copy-start.6
  566.3 3.7 copy-start.8
  572.8 2.4 copy-start.3
  572.8 2.4 copy-start.14
  572.8 2.4 copy-start.15
  572.8 2.4 copy-start.16
Sparse Core Ops, SparseCore 0:
  10.7 520.6 all-gather.1
  554.1 1195.0 all-reduce.15
where the time goes:
time: 1860 us
  waiting for transfers between devices  1690 us (91%)
  blocking collectives  103 us (6%)
  local copies, waits for them, and re-layouts  33.7 us (2%)
    unnamed x3, waiting for transfers between devices  1170 us
    all_gather x1, waiting for transfers between devices, body(): weight_full = lax.all_gather(conv_weight, 'shard', axis=1, tiled=True)  520 us
    psum x1, blocking collectives, body(): grad_weight = lax.psum(jnp.stack(blocks), 'rep')  103 us
  transfers between devices with their start and end apart: 2, of which 2 were waited for; matrix products, arithmetic and copies ran while one was open for 2% of the time, Pallas kernels for 0%

commit v1 on v0

v1 whole, which is shorter than its diff:
```python
import jax
import jax.numpy as jnp
from jax import lax
from jax.sharding import Mesh
from jax.sharding import PartitionSpec as P

GROUPS = 32
AXES = ("xh", "core", "z", "xl", "y")
SWAP = ((0, 0), (1, 2), (2, 1), (3, 3))


def norm_act(values, norm_gain, norm_bias):
    shape = values.shape
    per = shape[-1] // GROUPS
    grouped = values.reshape(shape[:-1] + (GROUPS, per))
    mean = jnp.mean(grouped, axis=(1, 2, 4), keepdims=True)
    centred = grouped - mean
    variance = jnp.mean(centred * centred, axis=(1, 2, 4), keepdims=True)
    normed = (centred / jnp.sqrt(variance + 1e-05)).reshape(shape) * norm_gain + norm_bias
    return jax.nn.silu(normed)


def spread(block, axis):
    count = lax.axis_size(axis)
    copies = jnp.broadcast_to(block[None], (count,) + block.shape)
    return lax.all_to_all(copies, axis, 0, 0, tiled=True)


def gather_weight(conv_weight, core):
    taps, rows, chans = conv_weight.shape
    block = lax.ppermute(conv_weight.reshape(taps * rows, chans), ("core", "xl"), SWAP)
    block = spread(block, "z")
    block = spread(block, "y")
    other = lax.ppermute(block, "core", ((0, 1), (1, 0)))
    low = jnp.where(core == 0, block, other)
    high = jnp.where(core == 0, other, block)
    full = jnp.stack([low, high])
    ys, zs = full.shape[1:3]
    full = full.reshape(2, ys, zs, taps, rows, chans).transpose(3, 2, 0, 1, 4, 5)
    return full.reshape(taps, zs * 2 * ys * rows, chans)


def reduce_terms(terms, core):
    taps, total, chans = terms.shape
    ys, zs = lax.axis_size("y"), lax.axis_size("z")
    rows = total // (2 * ys * zs)
    parts = terms.reshape(taps, zs, 2, ys, rows, chans).transpose(2, 3, 1, 0, 4, 5)
    parts = parts.reshape(2, ys, zs, taps * rows, chans)
    keep = jnp.where(core == 0, parts[0], parts[1])
    send = jnp.where(core == 0, parts[1], parts[0]).astype(jnp.bfloat16)
    got = lax.ppermute(send, "core", ((0, 1), (1, 0)))
    own = (keep + got.astype(jnp.float32)).astype(jnp.bfloat16)
    own = lax.all_to_all(own, "y", 0, 0, tiled=True).astype(jnp.float32).sum(0)
    own = lax.all_to_all(own.astype(jnp.bfloat16), "z", 0, 0, tiled=True)
    own = own.astype(jnp.float32).sum(0)
    own = spread(own, ("xh", "xl")).sum(0)
    return lax.ppermute(own, ("core", "xl"), SWAP).reshape(taps, rows, chans)


def body(latents, norm_gain, norm_bias, conv_weight, cotangent):
    count, rows, cols, chans = latents.shape
    scale = 1.0 / (count * lax.axis_size(AXES))
    core = lax.axis_index("core")
    cells = count * rows * cols
    weight_full = gather_weight(conv_weight, core)
    values = latents.astype(jnp.float32)
    activated = norm_act(values, norm_gain, norm_bias).astype(jnp.bfloat16)
    padded = jnp.pad(activated, ((0, 0), (1, 1), (1, 1), (0, 0)))
    flat_up = cotangent.reshape(cells, chans)
    pre = jnp.zeros((cells, chans), jnp.float32)
    total = jnp.zeros((count, rows + 2, cols + 2, chans), jnp.float32)
    patch_rows = []
    for i in range(3):
        taps = [padded[:, i : i + rows, j : j + cols, :] for j in range(3)]
        patches = jnp.concatenate(taps, axis=-1).reshape(cells, 3 * chans)
        patch_rows.append(patches)
    terms = jnp.stack(
        [jnp.einsum("pk,pc->kc", p, flat_up, preferred_element_type=jnp.float32) for p in patch_rows]
    )
    grad_weight = reduce_terms(terms, core) * scale
    for i in range(3):
        pre = pre + jnp.dot(patch_rows[i], weight_full[i], preferred_element_type=jnp.float32)
        patch_grad = jnp.einsum(
            "pc,kc->pk", flat_up, weight_full[i], preferred_element_type=jnp.float32
        )
        parts = patch_grad.reshape(count, rows, cols, 3, chans)
        for j in range(3):
            total = total + jnp.pad(parts[:, :, :, j, :], ((0, 0), (i, 2 - i), (j, 2 - j), (0, 0)))
    output = (values + pre.reshape(values.shape)).astype(jnp.bfloat16)
    act_grad = total[:, 1:-1, 1:-1, :]
    unused, pullback = jax.vjp(lambda v: norm_act(v, norm_gain, norm_bias), values)
    back = pullback(act_grad)[0]
    grad_input = (cotangent.astype(jnp.float32) + back).astype(jnp.bfloat16)
    return (output, grad_input, grad_weight)


def solution(mesh):
    fine = Mesh(mesh.devices.reshape(4, 2, 8, 2, 8), AXES)
    batch = P(("xh", "core", "z", "xl", "y"), None, None, None)
    weight = P(None, ("z", "xl", "y"), None)
    return jax.shard_map(
        body,
        mesh=fine,
        in_specs=(batch, P(), P(), weight, batch),
        out_specs=(batch, batch, weight),
        check_vma=False,
    )
```

time: 1860 us -> 316 us (0.17)
  waiting for transfers between devices: 1690 us -> 49.8 us
  local copies, waits for them, and re-layouts: 33.7 us -> 126 us
  blocking collectives: 103 us -> 65.5 us
  starting transfers between devices: 0.08 us -> 28.1 us
    unnamed x3 -> x0, waiting for transfers between devices: 1170 us -> none
    all_gather x1 -> x0, waiting for transfers between devices: 520 us -> none  [body(): weight_full = lax.all_gather(conv_weight, 'shard', axis=1, tiled=True)]
    psum x1 -> x0, blocking collectives: 103 us -> none  [body(): grad_weight = lax.psum(jnp.stack(blocks), 'rep')]
    all_to_all x0 -> x2, blocking collectives: none -> 65.5 us  [spread(): return lax.all_to_all(copies, axis, 0, 0, tiled=True)]
    another operation x3, local copies, waits for them, and re-layouts: 2.32 us -> 57.2 us  [body(): grad_weight = lax.psum(jnp.stack(blocks), 'rep')]
    all_to_all x0 -> x3, waiting for transfers between devices: none -> 44.1 us  [the longest x1 28.3 us: reduce_terms(): own = lax.all_to_all(own, 'y', 0, 0, tiled=True).astype(jnp.float32).sum(0)]
    dot_general x0 -> x6, local copies, waits for them, and re-layouts: none -> 27.3 us  [body(): jnp.einsum('pk,pc->kc', p, flat_up, preferred_element_type=jnp.float32)]
  transfers between devices with their start and end apart: 2 -> 7, of which waited for: 2 -> 6; matrix products, arithmetic and copies ran while one was open for 2% -> 6% of each run, Pallas kernels for 0% -> 0%
where the time goes in v1:
time: 316 us; the launch traced here: 313 us
  local copies, waits for them, and re-layouts  126 us (40%)
  blocking collectives  65.5 us (21%)
  waiting for transfers between devices  49.8 us (16%)
  matrix products  29 us (9%)
  starting transfers between devices  28.1 us (9%)
  other arithmetic  13.8 us (4%)
    all_to_all x2, blocking collectives, spread(): return lax.all_to_all(copies, axis, 0, 0, tiled=True)  65.5 us
    another operation x3, local copies, waits for them, and re-layouts  57.2 us
    all_to_all x1, waiting for transfers between devices, reduce_terms(): own = lax.all_to_all(own, 'y', 0, 0, tiled=True).astype(jnp.float32).sum(0)  28.3 us
    dot_general x6, local copies, waits for them, and re-layouts, body(): jnp.einsum('pk,pc->kc', p, flat_up, preferred_element_type=jnp.float32)  27.3 us
    dot_general x3, matrix products, body(): jnp.einsum('pk,pc->kc', p, flat_up, preferred_element_type=jnp.float32)  16.5 us
    all_to_all x1, waiting for transfers between devices, spread(): return lax.all_to_all(copies, axis, 0, 0, tiled=True)  9.04 us
    reshape x3, local copies, waits for them, and re-layouts, body(): parts = patch_grad.reshape(count, rows, cols, 3, chans)  8.69 us
    unnamed x66, local copies, waits for them, and re-layouts  7.93 us
  transfers between devices with their start and end apart: 7, of which 6 were waited for; matrix products, arithmetic and copies ran while one was open for 6% of the time, Pallas kernels for 0%

profile of v1, /device:TPU:1, one launch (start us, length us, event | category | flops | bytes accessed | tf_op | source)
XLA Modules:
  0.0 313.1 jit_solution(7920834815494722415)
XLA Ops:
  1.4 4.5 %collective-permute-start = (bf16[27,384]{1,0:T(8,128)(2,1)S(1)}, bf16[27,384]{1,0:T(8,128)(2,1)S(1)}, u32[]{:S(2)}, u32[]{:S(2)}) collective-permute-start(bf16[27,384]{1,0:T(8,128)(2,1)S(1)} %reshape.229), channel_id=1, source_target_pairs={{0,0},{8,128},{128,8},{136,136},{1,1},{9,129},{129,9},{137,137},{2... | collective-permute-start | bytes 62216 | tf_op jit(solution)/shard_map/ppermute | solution.py:31
  7.4 24.8 %all_to_all.25 = bf16[8,27,384]{2,1,0:T(8,128)(2,1)S(1)} all-to-all(bf16[8,27,384]{2,1,0:T(8,128)(2,1)S(1)} %broadcast_in_dim.20), channel_id=1, replica_groups=mesh['xh'=4,'core'=2,'z'=8,'xl'=2,'y'=8] {'z'}, dimensions={0} | all-to-all | bytes 331776 | tf_op jit(solution)/shard_map/all_to_all | solution.py:26
  32.5 40.6 %all_to_all.26 = bf16[8,8,27,384]{3,1,2,0:T(8,128)(2,1)S(1)} all-to-all(bf16[8,8,27,384]{3,1,2,0:T(8,128)(2,1)S(1)} %broadcast_in_dim.21), channel_id=1, replica_groups=mesh['xh'=4,'core'=2,'z'=8,'xl'=2,'y'=8] {'y'}, dimensions={0} | all-to-all | bytes 2654208 | tf_op jit(solution)/shard_map/all_to_all | solution.py:26
  89.2 2.8 reshape.233
  97.9 2.8 reshape.234
  100.7 3.0 fusion.27
  105.9 3.0 reshape.235
  117.8 6.9 %copy.178 = bf16[1152,24,20]{2,1,0:T(8,128)(2,1)} copy(bf16[1152,24,20]{0,2,1:T(8,128)(2,1)S(1)} %get-tuple-element.37) | data formatting | bytes 2211840 | tf_op jit(solution)/shard_map/pk,pc->kc/dot_general | solution.py:78
  124.7 19.1 %copy.179 = bf16[8,2,8,9,24,20]{4,3,5,2,1,0:T(8,128)(2,1)} copy(bf16[8,2,8,9,24,20]{5,4,3,2,1,0:T(8,128)(2,1)} %bitcast.91) | data formatting | bytes 2211840 | tf_op jit(solution)/shard_map/reshape.179
  143.8 5.3 %convolution_bitcast_fusion.5 = f32[8,2,8,9,384]{4,3,2,1,0:T(8,128)S(1)} fusion(bf16[8,2,8,9,24,20]{4,3,5,2,1,0:T(8,128)(2,1)} %copy.179, bf16[1,24,20,384]{3,1,2,0:T(8,128)(2,1)S(1)} %copy-done.27), kind=kOutput, calls=%fused_computation.10 | convolution fusion | flops 424673280 | bytes 3244032 | tf_op jit(solution)/shard_map/pk,pc->kc/dot_general | solution.py:78
  152.2 8.1 %copy.184 = bf16[1152,24,20]{2,1,0:T(8,128)(2,1)} copy(bf16[1152,24,20]{0,2,1:T(8,128)(2,1)} %get-tuple-element.39) | data formatting | bytes 2211840 | tf_op jit(solution)/shard_map/pk,pc->kc/dot_general | solution.py:78
  160.2 19.0 %copy.185 = bf16[8,2,8,9,24,20]{4,3,5,2,1,0:T(8,128)(2,1)} copy(bf16[8,2,8,9,24,20]{5,4,3,2,1,0:T(8,128)(2,1)} %bitcast.92) | data formatting | bytes 2211840 | tf_op jit(solution)/shard_map/reshape.183
  179.3 5.7 %convolution_bitcast_fusion.3 = f32[8,2,8,9,384]{4,3,2,1,0:T(8,128)S(1)} fusion(bf16[8,2,8,9,24,20]{4,3,5,2,1,0:T(8,128)(2,1)} %copy.185, bf16[1,24,20,384]{3,1,2,0:T(8,128)(2,1)} %param.9), kind=kOutput, calls=%fused_computation.8 | convolution fusion | flops 424673280 | bytes 3244032 | tf_op jit(solution)/shard_map/pk,pc->kc/dot_general | solution.py:78
  188.4 8.1 %copy.181 = bf16[1152,24,20]{2,1,0:T(8,128)(2,1)} copy(bf16[1152,24,20]{0,2,1:T(8,128)(2,1)} %maximum_bitcast_fusion.2) | data formatting | bytes 2211840 | tf_op jit(solution)/shard_map/pk,pc->kc/dot_general | solution.py:78
  196.5 19.0 %copy.182 = bf16[8,2,8,9,24,20]{4,3,5,2,1,0:T(8,128)(2,1)} copy(bf16[8,2,8,9,24,20]{5,4,3,2,1,0:T(8,128)(2,1)} %bitcast.93) | data formatting | bytes 2211840 | tf_op jit(solution)/shard_map/reshape.181
  215.6 5.4 %convolution_bitcast_fusion.4 = f32[8,2,8,9,384]{4,3,2,1,0:T(8,128)S(1)} fusion(bf16[8,2,8,9,24,20]{4,3,5,2,1,0:T(8,128)(2,1)} %copy.182, bf16[1,24,20,384]{3,1,2,0:T(8,128)(2,1)} %param.9), kind=kOutput, calls=%fused_computation.9 | convolution fusion | flops 424673280 | bytes 3244032 | tf_op jit(solution)/shard_map/pk,pc->kc/dot_general | solution.py:78
  229.5 4.4 %all-to-all-start.2 = ((bf16[8,8,27,384]{3,1,2,0:T(8,128)(2,1)}), bf16[8,8,27,384]{3,1,2,0:T(8,128)(2,1)}, u32[]{:S(2)}, u32[]{:S(2)}) async-start(bf16[8,8,27,384]{3,1,2,0:T(8,128)(2,1)} %add_convert_fusion), calls=%async_computation.2 | async-start | bytes 2654208 | tf_op jit(solution)/shard_map/all_to_all | solution.py:53
  240.8 28.3 %all-to-all-done.2 = bf16[8,8,27,384]{3,1,2,0:T(8,128)(2,1)} async-done(((bf16[8,8,27,384]{3,1,2,0:T(8,128)(2,1)}), bf16[8,8,27,384]{3,1,2,0:T(8,128)(2,1)}, u32[]{:S(2)}, u32[]{:S(2)}) %all-to-all-start.2) | async-done | bytes 1327136 | tf_op jit(solution)/shard_map/all_to_all | solution.py:53
  271.3 3.4 %all-to-all-start.3 = ((bf16[8,27,384]{2,1,0:T(8,128)(2,1)}), bf16[8,27,384]{2,1,0:T(8,128)(2,1)S(1)}, u32[]{:S(2)}, u32[]{:S(2)}) async-start(bf16[8,27,384]{2,1,0:T(8,128)(2,1)} %copy.187), calls=%async_computation.3 | async-start | bytes 393216 | tf_op jit(solution)/shard_map/all_to_all | solution.py:54
  274.8 3.0 fusion.30
  277.7 6.7 %all-to-all-done.3 = bf16[8,27,384]{2,1,0:T(8,128)(2,1)S(1)} async-done(((bf16[8,27,384]{2,1,0:T(8,128)(2,1)}), bf16[8,27,384]{2,1,0:T(8,128)(2,1)S(1)}, u32[]{:S(2)}, u32[]{:S(2)}) %all-to-all-start.3) | async-done | bytes 165920 | tf_op jit(solution)/shard_map/all_to_all | solution.py:54
  285.3 6.5 %all-to-all-start.4 = ((f32[8,27,384]{2,1,0:T(8,128)}), f32[8,27,384]{2,1,0:T(8,128)S(1)}, u32[]{:S(2)}, u32[]{:S(2)}) async-start(f32[8,27,384]{2,1,0:T(8,128)} %broadcast_in_dim.54), calls=%async_computation.4 | async-start | bytes 786432 | tf_op jit(solution)/shard_map/all_to_all | solution.py:26
  295.0 9.0 %all-to-all-done.4 = f32[8,27,384]{2,1,0:T(8,128)S(1)} async-done(((f32[8,27,384]{2,1,0:T(8,128)}), f32[8,27,384]{2,1,0:T(8,128)S(1)}, u32[]{:S(2)}, u32[]{:S(2)}) %all-to-all-start.4) | async-done | bytes 331808 | tf_op jit(solution)/shard_map/all_to_all | solution.py:26
  304.1 5.4 %collective-permute-start.3 = (f32[27,384]{1,0:T(8,128)S(1)}, f32[27,384]{1,0:T(8,128)S(1)}, u32[]{:S(2)}, u32[]{:S(2)}) collective-permute-start(f32[27,384]{1,0:T(8,128)S(1)} %reduce_sum.124), channel_id=1, source_target_pairs={{0,0},{8,128},{128,8},{136,136},{1,1},{9,129},{129,9},{137,137},{2... | collective-permute-start | bytes 124424 | tf_op jit(solution)/shard_map/ppermute | solution.py:57
  (149 shorter events, 66.7 us)
Async XLA Ops:
  1.4 6.0 %collective-permute-start = (bf16[27,384]{1,0:T(8,128)(2,1)S(1)}, bf16[27,384]{1,0:T(8,128)(2,1)S(1)}, u32[]{:S(2)}, u32[]{:S(2)}) collective-permute-start(bf16[27,384]{1,0:T(8,128)(2,1)S(1)} %reshape.229), channel_id=1, source_target_pairs={{0,0},{8,128},{128,8},{136,136},{1,1},{9,129},{129,9},{137,137},{2... | collective-permute-start | bytes 62216 | tf_op jit(solution)/shard_map/ppermute | solution.py:31
  32.3 42.7 %copy-start = (bf16[1,24,20,384]{3,1,2,0:T(8,128)(2,1)S(1)}, bf16[1,24,20,384]{3,1,2,0:T(8,128)(2,1)}, u32[]{:S(2)}) copy-start(bf16[1,24,20,384]{3,1,2,0:T(8,128)(2,1)} %param.5) | copy-start | bytes 1105924
  32.3 44.0 %copy-start.26 = (bf16[1,24,20,384]{3,1,2,0:T(8,128)(2,1)S(1)}, bf16[1,24,20,384]{3,1,2,0:T(8,128)(2,1)}, u32[]{:S(2)}) copy-start(bf16[1,24,20,384]{3,1,2,0:T(8,128)(2,1)} %param.9) | copy-start | bytes 1105924
  73.1 5.1 %collective-permute-start.1 = (bf16[8,8,27,384]{3,1,2,0:T(8,128)(2,1)S(1)}, bf16[8,8,27,384]{3,1,2,0:T(8,128)(2,1)}, u32[]{:S(2)}, u32[]{:S(2)}) collective-permute-start(bf16[8,8,27,384]{3,1,2,0:T(8,128)(2,1)S(1)} %all_to_all.26), channel_id=1, source_target_pairs={{0,128},{128,0},{1,129},{129,1},{2,130},{130,2},{3,131},{131,3},{4... | collective-permute-start | bytes 3981320 | tf_op jit(solution)/shard_map/ppermute | solution.py:34
  76.5 9.6 %copy-start.4 = (bf16[480,384]{1,0:T(8,128)(2,1)}, bf16[480,384]{1,0:T(8,128)(2,1)S(1)}, u32[]{:S(2)}) copy-start(bf16[480,384]{1,0:T(8,128)(2,1)S(1)} %reshape.232) | copy-start | bytes 1105924
  92.0 3.7 %copy-start.5 = (bf16[480,384]{1,0:T(8,128)(2,1)S(1)}, bf16[480,384]{1,0:T(8,128)(2,1)}, u32[]{:S(2)}) copy-start(bf16[480,384]{1,0:T(8,128)(2,1)} %copy-done.4) | copy-start | bytes 1105924
  92.0 3.6 %copy-start.14 = (bf16[1152,384]{1,0:T(8,128)(2,1)S(1)}, bf16[1152,384]{1,0:T(8,128)(2,1)}, u32[]{:S(2)}) copy-start(bf16[1152,384]{1,0:T(8,128)(2,1)} %squeeze.44) | copy-start | bytes 2654212
  100.7 3.0 copy-start.1
  100.7 3.0 copy-start.6
  124.7 19.1 %copy-start.27 = (bf16[1,24,20,384]{3,1,2,0:T(8,128)(2,1)S(1)}, bf16[1,24,20,384]{3,1,2,0:T(8,128)(2,1)}, u32[]{:S(2)}) copy-start(bf16[1,24,20,384]{3,1,2,0:T(8,128)(2,1)} %param.9) | copy-start | bytes 1105924
  185.0 2.3 copy-start.9
  185.0 2.3 copy-start.11
  223.2 5.0 %collective-permute-start.2 = (bf16[8,8,27,384]{3,1,2,0:T(8,128)(2,1)S(1)}, bf16[8,8,27,384]{3,1,2,0:T(8,128)(2,1)S(1)}, u32[]{:S(2)}, u32[]{:S(2)}) collective-permute-start(bf16[8,8,27,384]{3,1,2,0:T(8,128)(2,1)S(1)} %bitcast.101), channel_id=1, source_target_pairs={{0,128},{128,0},{1,129},{129,1},{2,130},{130,2},{3,131},{131,3},{4... | collective-permute-start | bytes 3981320 | tf_op jit(solution)/shard_map/ppermute | solution.py:51
  229.5 5.2 %copy-start.12 = (bf16[1,24,20,384]{3,2,1,0:T(8,128)(2,1)S(1)}, bf16[1,24,20,384]{3,2,1,0:T(8,128)(2,1)}, u32[]{:S(2)}) copy-start(bf16[1,24,20,384]{3,2,1,0:T(8,128)(2,1)} %get-tuple-element.44) | copy-start | bytes 1105924
  229.5 6.0 %copy-start.10 = (bf16[1,24,20,384]{3,2,1,0:T(8,128)(2,1)S(1)}, bf16[1,24,20,384]{3,2,1,0:T(8,128)(2,1)}, u32[]{:S(2)}) copy-start(bf16[1,24,20,384]{3,2,1,0:T(8,128)(2,1)} %get-tuple-element.45) | copy-start | bytes 1105924
  229.5 39.6 %all-to-all-start.2 = ((bf16[8,8,27,384]{3,1,2,0:T(8,128)(2,1)}), bf16[8,8,27,384]{3,1,2,0:T(8,128)(2,1)}, u32[]{:S(2)}, u32[]{:S(2)}) async-start(bf16[8,8,27,384]{3,1,2,0:T(8,128)(2,1)} %add_convert_fusion), calls=%async_computation.2 | async-start | bytes 2654208 | tf_op jit(solution)/shard_map/all_to_all | solution.py:53
  235.6 4.1 %copy-start.7 = (bf16[1,24,20,1152]{3,2,1,0:T(8,128)(2,1)S(1)}, bf16[1,24,20,1152]{3,2,1,0:T(8,128)(2,1)}, u32[]{:S(2)}) copy-start(bf16[1,24,20,1152]{3,2,1,0:T(8,128)(2,1)} %get-tuple-element.38) | copy-start | bytes 3317764
  239.7 35.0 %copy-start.17 = (bf16[1152,384]{1,0:T(8,128)(2,1)S(1)}, bf16[1152,384]{1,0:T(8,128)(2,1)}, u32[]{:S(2)}) copy-start(bf16[1152,384]{1,0:T(8,128)(2,1)} %copy-done.16) | copy-start | bytes 2654212
  271.3 13.1 %all-to-all-start.3 = ((bf16[8,27,384]{2,1,0:T(8,128)(2,1)}), bf16[8,27,384]{2,1,0:T(8,128)(2,1)S(1)}, u32[]{:S(2)}, u32[]{:S(2)}) async-start(bf16[8,27,384]{2,1,0:T(8,128)(2,1)} %copy.187), calls=%async_computation.3 | async-start | bytes 393216 | tf_op jit(solution)/shard_map/all_to_all | solution.py:54
  274.8 17.0 %copy-start.15 = (bf16[1152,384]{1,0:T(8,128)(2,1)S(1)}, bf16[1152,384]{1,0:T(8,128)(2,1)}, u32[]{:S(2)}) copy-start(bf16[1152,384]{1,0:T(8,128)(2,1)} %squeeze.44) | copy-start | bytes 2654212
  285.3 18.8 %all-to-all-start.4 = ((f32[8,27,384]{2,1,0:T(8,128)}), f32[8,27,384]{2,1,0:T(8,128)S(1)}, u32[]{:S(2)}, u32[]{:S(2)}) async-start(f32[8,27,384]{2,1,0:T(8,128)} %broadcast_in_dim.54), calls=%async_computation.4 | async-start | bytes 786432 | tf_op jit(solution)/shard_map/all_to_all | solution.py:26
  291.8 2.4 copy-start.2
  291.8 2.4 copy-start.8
  304.1 8.3 %collective-permute-start.3 = (f32[27,384]{1,0:T(8,128)S(1)}, f32[27,384]{1,0:T(8,128)S(1)}, u32[]{:S(2)}, u32[]{:S(2)}) collective-permute-start(f32[27,384]{1,0:T(8,128)S(1)} %reduce_sum.124), channel_id=1, source_target_pairs={{0,0},{8,128},{128,8},{136,136},{1,1},{9,129},{129,9},{137,137},{2... | collective-permute-start | bytes 124424 | tf_op jit(solution)/shard_map/ppermute | solution.py:57
  (13 other events, 16.5 us)

commit v2 on v1

v2 whole, which is shorter than its diff:
```python
import functools

import jax
import jax.numpy as jnp
import numpy as np
from jax import lax
from jax.experimental import pallas as pl
from jax.experimental.pallas import tpu as pltpu
from jax.sharding import Mesh
from jax.sharding import PartitionSpec as P

GROUPS = 32
HEIGHT, WIDTH, CHANS = 24, 20, 384
CELLS = HEIGHT * WIDTH
PER = CHANS // GROUPS
TOP = 24
ROWS = 9
YS, ZS = 8, 8
PACK = 224
ZROWS = 2 * YS * ROWS
AXES = ("xh", "core", "z", "xl", "y")
SWAP = ((0, 0), (1, 2), (2, 1), (3, 3))
VMEM_LIMIT = 40 * 1024 * 1024


def placement():
    sel = np.zeros((2, PACK, 3 * ZROWS), np.float32)
    for half in range(2):
        for y in range(YS):
            for i in range(3):
                for r in range(ROWS):
                    row = (half * YS + y) * ROWS + r
                    sel[half, (y * 3 + i) * ROWS + r, i * ZROWS + row] = 1.0
    return sel


SEL = placement()


def dot(a, b, dims=((1,), (0,))):
    return lax.dot_general(a, b, (dims, ((), ())), preferred_element_type=jnp.float32)


def group_mean(row):
    a = lax.broadcasted_iota(jnp.int32, (CHANS, GROUPS), 0)
    b = lax.broadcasted_iota(jnp.int32, (CHANS, GROUPS), 1) * PER
    member = jnp.where((a >= b) & (a < b + PER), 1.0, 0.0).astype(jnp.float32)
    total = lax.dot_general(
        row, member, (((1,), (0,)), ((), ())),
        precision=lax.Precision.HIGHEST, preferred_element_type=jnp.float32,
    )
    back = lax.dot_general(
        total, member, (((1,), (1,)), ((), ())),
        precision=lax.Precision.HIGHEST, preferred_element_type=jnp.float32,
    )
    return back * (1.0 / (CELLS * PER))


def channel_sum(values):
    return jnp.broadcast_to(jnp.sum(values, axis=0, keepdims=True), (8, CHANS))


def flatten(ref, flat):
    for h in range(HEIGHT):
        flat[h * WIDTH : (h + 1) * WIDTH, :] = ref[0, h].astype(jnp.float32)


def statistics(flat):
    mean = group_mean(channel_sum(flat[...]))[0:1]
    centred = flat[...] - mean
    variance = group_mean(channel_sum(centred * centred))[0:1]
    return mean, 1.0 / jnp.sqrt(variance + 1e-05)


def build_patches(shifted, patches):
    col = lax.broadcasted_iota(jnp.int32, (CELLS, CHANS), 0) % WIDTH
    for i in range(3):
        for j in range(3):
            start = TOP + (i - 1) * WIDTH + (j - 1)
            tap = shifted[start : start + CELLS, :]
            if j == 0:
                tap = jnp.where(col == 0, 0.0, tap)
            if j == 2:
                tap = jnp.where(col == WIDTH - 1, 0.0, tap)
            at = (i * 3 + j) * CHANS
            patches[:, at : at + CHANS] = tap.astype(jnp.bfloat16)


def clear_edges(shifted):
    edge = jnp.zeros((TOP, CHANS), jnp.float32)
    shifted[:TOP, :] = edge
    shifted[TOP + CELLS :, :] = edge


def activate(flat, gain, bias, shifted):
    mean, inverse = statistics(flat)
    normed = (flat[...] - mean) * inverse * gain[...] + bias[...]
    active = normed / (1.0 + jnp.exp(-normed))
    shifted[TOP : TOP + CELLS, :] = active.astype(jnp.bfloat16).astype(jnp.float32)
    return mean, inverse


def term_kernel(core, lat, gain, bias, cot, sel, keep, send, flat, shifted, up, patches, terms):
    clear_edges(shifted)
    flatten(cot, flat)
    up[...] = flat[...].astype(jnp.bfloat16)
    flatten(lat, flat)
    activate(flat, gain, bias, shifted)
    build_patches(shifted, patches)
    for t in range(9):
        at = t * CHANS
        terms[at : at + CHANS, :] = dot(patches[:, at : at + CHANS], up[...], ((0,), (0,)))
    mine, other = sel[core[0]], sel[1 - core[0]]
    for z in range(ZS):
        block = jnp.concatenate(
            [terms[i * 3 * CHANS + z * ZROWS : i * 3 * CHANS + (z + 1) * ZROWS, :] for i in range(3)]
        )
        high = block.astype(jnp.bfloat16)
        low = (block - high.astype(jnp.float32)).astype(jnp.bfloat16)
        keep[z] = dot(mine, high) + dot(mine, low)
        send[z] = dot(other, high).astype(jnp.bfloat16)


def layer_kernel(
    core, lat, gain, bias, cot, held, got, sel, out, grad, flat, shifted, up, patches, weight
):
    clear_edges(shifted)
    flatten(cot, up)
    flatten(lat, flat)
    mean, inverse = activate(flat, gain, bias, shifted)
    build_patches(shifted, patches)
    mine, other = sel[core[0]], sel[1 - core[0]]
    for z in range(ZS):
        block = dot(mine, held[z], ((0,), (0,))) + dot(other, got[z], ((0,), (0,)))
        for i in range(3):
            at = i * 3 * CHANS + z * ZROWS
            weight[at : at + ZROWS, :] = block[i * ZROWS : (i + 1) * ZROWS].astype(jnp.bfloat16)
    result = dot(patches[...], weight[...]) + flat[...]
    shifted[TOP : TOP + CELLS, :] = up[...]
    for h in range(HEIGHT):
        out[0, h] = result[h * WIDTH : (h + 1) * WIDTH].astype(jnp.bfloat16)
    build_patches(shifted, patches)
    back = jnp.zeros((CELLS, CHANS), jnp.float32)
    for t in range(9):
        at, mirror = t * CHANS, (8 - t) * CHANS
        back = back + dot(
            patches[:, mirror : mirror + CHANS], weight[at : at + CHANS, :], ((1,), (1,))
        )
    hat = (flat[...] - mean) * inverse
    normed = hat * gain[...] + bias[...]
    gate = 1.0 / (1.0 + jnp.exp(-normed))
    back = back * (gate * (1.0 + normed * (1.0 - gate))) * gain[...]
    first = group_mean(channel_sum(back))[0:1]
    second = group_mean(channel_sum(back * hat))[0:1]
    result = up[...] + inverse * (back - first - hat * second)
    for h in range(HEIGHT):
        grad[0, h] = result[h * WIDTH : (h + 1) * WIDTH].astype(jnp.bfloat16)


VMEM = functools.partial(pl.BlockSpec, memory_space=pltpu.VMEM)
SMEM = functools.partial(pl.BlockSpec, memory_space=pltpu.SMEM)


def spread(block, axis):
    count = lax.axis_size(axis)
    copies = jnp.broadcast_to(block[None], (count,) + block.shape)
    return lax.all_to_all(copies, axis, 0, 0, tiled=True)


def gather_halves(conv_weight):
    taps, rows, chans = conv_weight.shape
    block = lax.ppermute(conv_weight.reshape(taps * rows, chans), ("core", "xl"), SWAP)
    block = spread(block, "y").reshape(YS * taps * rows, chans)
    block = jnp.pad(block, ((0, PACK - YS * taps * rows), (0, 0)))
    held = spread(block, "z")
    return held, lax.ppermute(held, "core", ((0, 1), (1, 0)))


def reduce_terms(keep, send):
    got = lax.ppermute(send, "core", ((0, 1), (1, 0)))
    own = (keep + got.astype(jnp.float32)).astype(jnp.bfloat16)
    own = lax.all_to_all(own, "z", 0, 0, tiled=True).astype(jnp.float32).sum(0)
    own = own[: YS * 3 * ROWS].reshape(YS, 3 * ROWS, CHANS).astype(jnp.bfloat16)
    own = lax.all_to_all(own, "y", 0, 0, tiled=True).astype(jnp.float32).sum(0)
    own = spread(own, ("xh", "xl")).sum(0)
    return lax.ppermute(own, ("core", "xl"), SWAP).reshape(3, ROWS, CHANS)


def terms_of(core, latents, gain, bias, cotangent, sel, **options):
    packed = (ZS, PACK, CHANS)
    return pl.pallas_call(
        term_kernel,
        out_shape=(
            jax.ShapeDtypeStruct(packed, jnp.float32),
            jax.ShapeDtypeStruct(packed, jnp.bfloat16),
        ),
        in_specs=[SMEM()] + [VMEM()] * 5,
        out_specs=(VMEM(), VMEM()),
        scratch_shapes=[
            pltpu.VMEM((CELLS, CHANS), jnp.float32),
            pltpu.VMEM((CELLS + 2 * TOP, CHANS), jnp.float32),
            pltpu.VMEM((CELLS, CHANS), jnp.bfloat16),
            pltpu.VMEM((CELLS, 9 * CHANS), jnp.bfloat16),
            pltpu.VMEM((9 * CHANS, CHANS), jnp.float32),
        ],
        compiler_params=pltpu.CompilerParams(vmem_limit_bytes=VMEM_LIMIT),
        cost_estimate=pl.CostEstimate(
            flops=4 * 10**9, bytes_accessed=8 * 10**6, transcendentals=CELLS * CHANS
        ),
        **options,
    )(core, latents, gain, bias, cotangent, sel)


def layer_of(core, latents, gain, bias, cotangent, held, got, sel, **options):
    return pl.pallas_call(
        layer_kernel,
        out_shape=(
            jax.ShapeDtypeStruct(latents.shape, jnp.bfloat16),
            jax.ShapeDtypeStruct(latents.shape, jnp.bfloat16),
        ),
        in_specs=[SMEM()] + [VMEM()] * 7,
        out_specs=(VMEM(), VMEM()),
        scratch_shapes=[
            pltpu.VMEM((CELLS, CHANS), jnp.float32),
            pltpu.VMEM((CELLS + 2 * TOP, CHANS), jnp.float32),
            pltpu.VMEM((CELLS, CHANS), jnp.float32),
            pltpu.VMEM((CELLS, 9 * CHANS), jnp.bfloat16),
            pltpu.VMEM((9 * CHANS, CHANS), jnp.bfloat16),
        ],
        compiler_params=pltpu.CompilerParams(vmem_limit_bytes=VMEM_LIMIT),
        cost_estimate=pl.CostEstimate(
            flops=4 * 10**9, bytes_accessed=8 * 10**6, transcendentals=2 * CELLS * CHANS
        ),
        **options,
    )(core, latents, gain, bias, cotangent, held, got, sel)


def body(latents, norm_gain, norm_bias, conv_weight, cotangent):
    scale = 1.0 / (latents.shape[0] * lax.axis_size(AXES))
    core = lax.axis_index("core").reshape(1)
    gain, bias = norm_gain[None], norm_bias[None]
    sel = jnp.asarray(SEL, jnp.bfloat16)
    held, got = gather_halves(conv_weight)
    keep, send = terms_of(core, latents, gain, bias, cotangent, sel)
    grad_weight = reduce_terms(keep, send) * scale
    output, grad_input = layer_of(core, latents, gain, bias, cotangent, held, got, sel)
    return (output, grad_input, grad_weight)


def solution(mesh):
    fine = Mesh(mesh.devices.reshape(4, 2, 8, 2, 8), AXES)
    batch = P(("xh", "core", "z", "xl", "y"), None, None, None)
    weight = P(None, ("z", "xl", "y"), None)
    return jax.shard_map(
        body,
        mesh=fine,
        in_specs=(batch, P(), P(), weight, batch),
        out_specs=(batch, batch, weight),
        check_vma=False,
    )
```

time: 316 us -> 168 us (0.53)
  local copies, waits for them, and re-layouts: 126 us -> 5.36 us
  matrix products: 29 us -> 0 us
  blocking collectives: 65.5 us -> 45.8 us
  Pallas kernels: 0 us -> 17.6 us
  other arithmetic: 13.8 us -> 3.03 us
  waiting for transfers between devices: 49.8 us -> 58.7 us
  starting transfers between devices: 28.1 us -> 35.9 us
    another operation x3 -> x0, local copies, waits for them, and re-layouts: 57.2 us -> none
    all_to_all x2, blocking collectives: 65.5 us -> 33.7 us  [spread(): return lax.all_to_all(copies, axis, 0, 0, tiled=True)]
    dot_general x9 -> x0, matrix products: 29 us -> none  [the longest x3 16.5 us: body(): jnp.einsum('pk,pc->kc', p, flat_up, preferred_element_type=jnp.float32)]
    dot_general x6 -> x0, local copies, waits for them, and re-layouts: 27.3 us -> none  [body(): jnp.einsum('pk,pc->kc', p, flat_up, preferred_element_type=jnp.float32)]
    pallas_call x0 -> x2, Pallas kernels: none -> 17.6 us  [the longest x1 10.5 us: layer_of(): pl.pallas_call(layer_kernel, out_shape=(jax.ShapeDtypeStruct(latents.shap...]
    reshape x8 -> x2, local copies, waits for them, and re-layouts: 12.2 us -> 0.08 us  [the longest x1 0.07 us: gather_halves(): block = spread(block, 'y').reshape(YS * taps * rows, chans)]
    all_to_all x0 -> x1, blocking collectives: none -> 12.1 us  [reduce_terms(): own = lax.all_to_all(own, 'y', 0, 0, tiled=True).astype(jnp.float32).sum(0)]
    slice x8 -> x1, local copies, waits for them, and re-layouts: 12 us -> 0.02 us  [reduce_terms(): own = own[:YS * 3 * ROWS].reshape(YS, 3 * ROWS, CHANS).astype(jnp.bfloat16)]
  transfers between devices with their start and end apart: 7 -> 6, of which waited for: 6 -> 4; matrix products, arithmetic and copies ran while one was open for 6% -> 3% of each run, Pallas kernels for 0% -> 11%
where the time goes in v2:
time: 168 us; the launch traced here: 167 us
  waiting for transfers between devices  58.7 us (35%)
  blocking collectives  45.8 us (27%)
  starting transfers between devices  35.9 us (21%)
  Pallas kernels  17.6 us (10%)
  local copies, waits for them, and re-layouts  5.36 us (3%)
  other arithmetic  3.03 us (2%)
    all_to_all x1, waiting for transfers between devices, reduce_terms(): own = lax.all_to_all(own, 'z', 0, 0, tiled=True).astype(jnp.float32).sum(0)  33.9 us
    all_to_all x2, blocking collectives, spread(): return lax.all_to_all(copies, axis, 0, 0, tiled=True)  33.7 us
    all_to_all x1, waiting for transfers between devices, spread(): return lax.all_to_all(copies, axis, 0, 0, tiled=True)  20.2 us
    all_to_all x1, starting transfers between devices, spread(): return lax.all_to_all(copies, axis, 0, 0, tiled=True)  16.5 us
    all_to_all x1, blocking collectives, reduce_terms(): own = lax.all_to_all(own, 'y', 0, 0, tiled=True).astype(jnp.float32).sum(0)  12.1 us
    pallas_call x1, Pallas kernels, layer_of(): pl.pallas_call(layer_kernel, out_shape=(jax.ShapeDtypeStruct(latents.shap...  10.5 us
    pallas_call x1, Pallas kernels, terms_of(): pl.pallas_call(term_kernel, out_shape=(jax.ShapeDtypeStruct(packed, jnp.f...  7.04 us
    ppermute x1, starting transfers between devices, reduce_terms(): return lax.ppermute(own, ('core', 'xl'), SWAP).reshape(3, ROWS, CHANS)  6.3 us
  transfers between devices with their start and end apart: 6, of which 4 were waited for; matrix products, arithmetic and copies ran while one was open for 3% of the time, Pallas kernels for 11%

profile of v2, /device:TPU:1, one launch (start us, length us, event | category | flops | bytes accessed | tf_op | source)
XLA Modules:
  0.0 167.1 jit_solution(14991406816915545537)
XLA Ops:
  0.6 0.8 copy.31
  1.4 4.5 %collective-permute-start = (bf16[27,384]{1,0:T(8,128)(2,1)S(1)}, bf16[27,384]{1,0:T(8,128)(2,1)S(1)}, u32[]{:S(2)}, u32[]{:S(2)}) collective-permute-start(bf16[27,384]{1,0:T(8,128)(2,1)S(1)} %reshape.24), channel_id=1, source_target_pairs={{0,0},{8,128},{128,8},{136,136},{1,1},{9,129},{129,9},{137,137},{2... | collective-permute-start | bytes 62216 | tf_op jit(solution)/shard_map/ppermute | solution.py:172
  5.9 1.5 collective-permute-done
  7.4 15.7 %all_to_all.25 = bf16[8,27,384]{2,1,0:T(8,128)(2,1)S(1)} all-to-all(bf16[8,27,384]{2,1,0:T(8,128)(2,1)S(1)} %broadcast_in_dim.12), channel_id=1, replica_groups=mesh['xh'=4,'core'=2,'z'=8,'xl'=2,'y'=8] {'y'}, dimensions={0} | all-to-all | bytes 331776 | tf_op jit(solution)/shard_map/all_to_all | solution.py:167
  23.2 0.1 reshape.25
  23.3 1.2 broadcast_in_dim.13
  24.5 16.5 %all-to-all-start.1 = ((bf16[8,224,384]{2,1,0:T(8,128)(2,1)}), bf16[8,224,384]{2,1,0:T(8,128)(2,1)S(1)}, u32[]{:S(2)}, u32[]{:S(2)}) async-start(bf16[8,224,384]{2,1,0:T(8,128)(2,1)} %broadcast_in_dim.13), calls=%async_computation.1 | async-start | bytes 2752512 | tf_op jit(solution)/shard_map/all_to_all | solution.py:167
  41.2 0.8 copy-done
  42.0 7.0 %shard_map.86 = (f32[8,224,384]{2,1,0:T(8,128)S(1)}, bf16[8,224,384]{2,1,0:T(8,128)(2,1)S(1)}) custom-call(s32[1]{0:T(128)} %bitcast.core, bf16[1,24,20,384]{3,2,1,0:T(8,128)(2,1)S(1)} %copy.32.lat, f32[1,384]{1,0:T(1,128)S(1)} %broadcast_in_dim.10.gain, f32[1,384]{1,0:T(1,128)S(1)} %broadcast_in_dim.11.bias, bf16[1,24,20,384]{3,2,1,0:T(8,128)(2,1)S(1)} %copy.33.cot, ...), custom_call_target="tpu_custom_call" | custom-call | flops 4000000000 | bytes 8000000 | tf_op jit(solution)/shard_map/pallas_call | solution.py:191
  49.1 1.9 %collective-permute-start.2 = (bf16[8,224,384]{2,1,0:T(8,128)(2,1)S(1)}, bf16[8,224,384]{2,1,0:T(8,128)(2,1)S(1)}, u32[]{:S(2)}, u32[]{:S(2)}) collective-permute-start(bf16[8,224,384]{2,1,0:T(8,128)(2,1)S(1)} %get-tuple-element.10), channel_id=1, source_target_pairs={{0,128},{128,0},{1,129},{129,1},{2,130},{130,2},{3,131},{131,3},{4... | collective-permute-start | bytes 4128776 | tf_op jit(solution)/shard_map/ppermute | solution.py:180
  51.0 3.1 %collective-permute-done.2 = bf16[8,224,384]{2,1,0:T(8,128)(2,1)S(1)} collective-permute-done((bf16[8,224,384]{2,1,0:T(8,128)(2,1)S(1)}, bf16[8,224,384]{2,1,0:T(8,128)(2,1)S(1)}, u32[]{:S(2)}, u32[]{:S(2)}) %collective-permute-start.2) | collective-permute-done | bytes 1376288 | tf_op jit(solution)/shard_map/ppermute | solution.py:180
  54.1 1.4 add_convert_fusion
  55.5 20.2 %all-to-all-done.1.held = bf16[8,224,384]{2,1,0:T(8,128)(2,1)S(1)} async-done(((bf16[8,224,384]{2,1,0:T(8,128)(2,1)}), bf16[8,224,384]{2,1,0:T(8,128)(2,1)S(1)}, u32[]{:S(2)}, u32[]{:S(2)}) %all-to-all-start.1) | async-done | bytes 1376288 | tf_op jit(solution)/shard_map/all_to_all | solution.py:167
  75.7 4.3 %all-to-all-start.2 = ((bf16[8,224,384]{2,1,0:T(8,128)(2,1)}), bf16[8,224,384]{2,1,0:T(8,128)(2,1)}, u32[]{:S(2)}, u32[]{:S(2)}) async-start(bf16[8,224,384]{2,1,0:T(8,128)(2,1)} %add_convert_fusion), calls=%async_computation.2 | async-start | bytes 2752512 | tf_op jit(solution)/shard_map/all_to_all | solution.py:182
  79.9 2.3 %collective-permute-start.1 = (bf16[8,224,384]{2,1,0:T(8,128)(2,1)S(1)}, bf16[8,224,384]{2,1,0:T(8,128)(2,1)}, u32[]{:S(2)}, u32[]{:S(2)}) collective-permute-start(bf16[8,224,384]{2,1,0:T(8,128)(2,1)S(1)} %all-to-all-done.1.held), channel_id=1, source_target_pairs={{0,128},{128,0},{1,129},{129,1},{2,130},{130,2},{3,131},{131,3},{4... | collective-permute-start | bytes 4128776 | tf_op jit(solution)/shard_map/ppermute | solution.py:176
  82.3 33.9 %all-to-all-done.2 = bf16[8,224,384]{2,1,0:T(8,128)(2,1)} async-done(((bf16[8,224,384]{2,1,0:T(8,128)(2,1)}), bf16[8,224,384]{2,1,0:T(8,128)(2,1)}, u32[]{:S(2)}, u32[]{:S(2)}) %all-to-all-start.2) | async-done | bytes 1376288 | tf_op jit(solution)/shard_map/all_to_all | solution.py:182
  116.2 1.5 reduce
  117.8 12.1 %all_to_all.26 = bf16[8,27,384]{2,1,0:T(8,128)(2,1)S(1)} all-to-all(bf16[8,27,384]{2,1,0:T(8,128)(2,1)S(1)} %convert_element_type.21), channel_id=1, replica_groups=mesh['xh'=4,'core'=2,'z'=8,'xl'=2,'y'=8] {'y'}, dimensions={0} | all-to-all | bytes 331776 | tf_op jit(solution)/shard_map/all_to_all | solution.py:184
  130.0 18.0 %all_to_all.27 = f32[8,27,384]{2,1,0:T(8,128)S(1)} all-to-all(f32[8,27,384]{2,1,0:T(8,128)S(1)} %broadcast_in_dim.28), channel_id=1, replica_groups=mesh['xh'=4,'core'=2,'z'=8,'xl'=2,'y'=8] {'xh','xl'}, dimensions={0} | all-to-all | bytes 663552 | tf_op jit(solution)/shard_map/all_to_all | solution.py:167
  148.0 6.3 %collective-permute-start.3 = (f32[27,384]{1,0:T(8,128)S(1)}, f32[27,384]{1,0:T(8,128)S(1)}, u32[]{:S(2)}, u32[]{:S(2)}) collective-permute-start(f32[27,384]{1,0:T(8,128)S(1)} %reduce_sum.29), channel_id=1, source_target_pairs={{0,0},{8,128},{128,8},{136,136},{1,1},{9,129},{129,9},{137,137},{2... | collective-permute-start | bytes 124424 | tf_op jit(solution)/shard_map/ppermute | solution.py:186
  154.4 10.5 %shard_map.85 = (bf16[1,24,20,384]{3,2,1,0:T(8,128)(2,1)S(1)}, bf16[1,24,20,384]{3,2,1,0:T(8,128)(2,1)S(1)}) custom-call(s32[1]{0:T(128)} %bitcast.core, bf16[1,24,20,384]{3,2,1,0:T(8,128)(2,1)S(1)} %copy.32.lat, f32[1,384]{1,0:T(1,128)S(1)} %broadcast_in_dim.10.gain, f32[1,384]{1,0:T(1,128)S(1)} %broadcast_in_dim.11.bias, ...), custom_call_target="tpu_custom_call" | custom-call | flops 4000000000 | bytes 8000000 | tf_op jit(solution)/shard_map/pallas_call | solution.py:215
  164.9 0.8 copy.37
  165.7 0.8 copy.38
  166.5 0.6 copy.39
  (25 shorter events, 0.4 us)
Async XLA Ops:
  1.4 6.0 %collective-permute-start = (bf16[27,384]{1,0:T(8,128)(2,1)S(1)}, bf16[27,384]{1,0:T(8,128)(2,1)S(1)}, u32[]{:S(2)}, u32[]{:S(2)}) collective-permute-start(bf16[27,384]{1,0:T(8,128)(2,1)S(1)} %reshape.24), channel_id=1, source_target_pairs={{0,0},{8,128},{128,8},{136,136},{1,1},{9,129},{129,9},{137,137},{2... | collective-permute-start | bytes 62216 | tf_op jit(solution)/shard_map/ppermute | solution.py:172
  24.5 16.6 %copy-start.3 = (f32[384]{0:T(512)S(1)}, f32[384]{0:T(512)}, u32[]{:S(2)}) copy-start(f32[384]{0:T(512)} %param.7) | copy-start | bytes 4612
  24.5 16.6 %copy-start.4 = (f32[384]{0:T(512)S(1)}, f32[384]{0:T(512)}, u32[]{:S(2)}) copy-start(f32[384]{0:T(512)} %param.8) | copy-start | bytes 4612
  24.5 16.6 %copy-start.1 = (bf16[1,24,20,384]{3,1,2,0:T(8,128)(2,1)S(1)}, bf16[1,24,20,384]{3,1,2,0:T(8,128)(2,1)}, u32[]{:S(2)}) copy-start(bf16[1,24,20,384]{3,1,2,0:T(8,128)(2,1)} %param.6) | copy-start | bytes 1105924
  24.5 16.7 %copy-start.2 = (bf16[1,24,20,384]{3,1,2,0:T(8,128)(2,1)S(1)}, bf16[1,24,20,384]{3,1,2,0:T(8,128)(2,1)}, u32[]{:S(2)}) copy-start(bf16[1,24,20,384]{3,1,2,0:T(8,128)(2,1)} %param.10) | copy-start | bytes 1105924
  24.5 51.2 %all-to-all-start.1 = ((bf16[8,224,384]{2,1,0:T(8,128)(2,1)}), bf16[8,224,384]{2,1,0:T(8,128)(2,1)S(1)}, u32[]{:S(2)}, u32[]{:S(2)}) async-start(bf16[8,224,384]{2,1,0:T(8,128)(2,1)} %broadcast_in_dim.13), calls=%async_computation.1 | async-start | bytes 2752512 | tf_op jit(solution)/shard_map/all_to_all | solution.py:167
  41.0 1.0 copy-start
  49.1 5.0 %collective-permute-start.2 = (bf16[8,224,384]{2,1,0:T(8,128)(2,1)S(1)}, bf16[8,224,384]{2,1,0:T(8,128)(2,1)S(1)}, u32[]{:S(2)}, u32[]{:S(2)}) collective-permute-start(bf16[8,224,384]{2,1,0:T(8,128)(2,1)S(1)} %get-tuple-element.10), channel_id=1, source_target_pairs={{0,128},{128,0},{1,129},{129,1},{2,130},{130,2},{3,131},{131,3},{4... | collective-permute-start | bytes 4128776 | tf_op jit(solution)/shard_map/ppermute | solution.py:180
  75.7 40.5 %all-to-all-start.2 = ((bf16[8,224,384]{2,1,0:T(8,128)(2,1)}), bf16[8,224,384]{2,1,0:T(8,128)(2,1)}, u32[]{:S(2)}, u32[]{:S(2)}) async-start(bf16[8,224,384]{2,1,0:T(8,128)(2,1)} %add_convert_fusion), calls=%async_computation.2 | async-start | bytes 2752512 | tf_op jit(solution)/shard_map/all_to_all | solution.py:182
  79.9 74.4 %collective-permute-start.1 = (bf16[8,224,384]{2,1,0:T(8,128)(2,1)S(1)}, bf16[8,224,384]{2,1,0:T(8,128)(2,1)}, u32[]{:S(2)}, u32[]{:S(2)}) collective-permute-start(bf16[8,224,384]{2,1,0:T(8,128)(2,1)S(1)} %all-to-all-done.1.held), channel_id=1, source_target_pairs={{0,128},{128,0},{1,129},{129,1},{2,130},{130,2},{3,131},{131,3},{4... | collective-permute-start | bytes 4128776 | tf_op jit(solution)/shard_map/ppermute | solution.py:176
  148.0 18.4 %collective-permute-start.3 = (f32[27,384]{1,0:T(8,128)S(1)}, f32[27,384]{1,0:T(8,128)S(1)}, u32[]{:S(2)}, u32[]{:S(2)}) collective-permute-start(f32[27,384]{1,0:T(8,128)S(1)} %reduce_sum.29), channel_id=1, source_target_pairs={{0,0},{8,128},{128,8},{136,136},{1,1},{9,129},{129,9},{137,137},{2... | collective-permute-start | bytes 124424 | tf_op jit(solution)/shard_map/ppermute | solution.py:186

commit v3 on v2

--- a/solution.py
+++ b/solution.py
@@ -13,24 +13,30 @@
 HEIGHT, WIDTH, CHANS = 24, 20, 384
 CELLS = HEIGHT * WIDTH
 PER = CHANS // GROUPS
-TOP = 24
+TOP = 32
 ROWS = 9
 YS, ZS = 8, 8
-PACK = 224
+HIGH, LOW = 4, 2
+SLOT = 28
+QUAD = HIGH * SLOT
+PACKED = (LOW * LOW, HIGH, QUAD, CHANS)
 ZROWS = 2 * YS * ROWS
-AXES = ("xh", "core", "z", "xl", "y")
+AXES = ("xh", "core", "zh", "zl", "xl", "yh", "yl")
 SWAP = ((0, 0), (1, 2), (2, 1), (3, 3))
+NEAR = ((1, 0), (2, 3), (3, 1), (0, 2))
+TRADE = ((0, 1), (1, 0))
 VMEM_LIMIT = 40 * 1024 * 1024
 
 
 def placement():
-    sel = np.zeros((2, PACK, 3 * ZROWS), np.float32)
+    sel = np.zeros((2, LOW * QUAD, 3 * ZROWS), np.float32)
     for half in range(2):
         for y in range(YS):
+            slot = (y % LOW) * QUAD + (y // LOW) * SLOT
             for i in range(3):
                 for r in range(ROWS):
                     row = (half * YS + y) * ROWS + r
-                    sel[half, (y * 3 + i) * ROWS + r, i * ZROWS + row] = 1.0
+                    sel[half, slot + i * ROWS + r, i * ZROWS + row] = 1.0
     return sel
 
 
@@ -60,11 +66,6 @@
     return jnp.broadcast_to(jnp.sum(values, axis=0, keepdims=True), (8, CHANS))
 
 
-def flatten(ref, flat):
-    for h in range(HEIGHT):
-        flat[h * WIDTH : (h + 1) * WIDTH, :] = ref[0, h].astype(jnp.float32)
-
-
 def statistics(flat):
     mean = group_mean(channel_sum(flat[...]))[0:1]
     centred = flat[...] - mean
@@ -73,15 +74,15 @@
 
 
 def build_patches(shifted, patches):
-    col = lax.broadcasted_iota(jnp.int32, (CELLS, CHANS), 0) % WIDTH
+    row = lax.broadcasted_iota(jnp.int32, (CELLS, CHANS), 0) % HEIGHT
     for i in range(3):
         for j in range(3):
-            start = TOP + (i - 1) * WIDTH + (j - 1)
+            start = TOP + (j - 1) * HEIGHT + (i - 1)
             tap = shifted[start : start + CELLS, :]
-            if j == 0:
-                tap = jnp.where(col == 0, 0.0, tap)
-            if j == 2:
-                tap = jnp.where(col == WIDTH - 1, 0.0, tap)
+            if i == 0:
+                tap = jnp.where(row == 0, 0.0, tap)
+            if i == 2:
+                tap = jnp.where(row == HEIGHT - 1, 0.0, tap)
             at = (i * 3 + j) * CHANS
             patches[:, at : at + CHANS] = tap.astype(jnp.bfloat16)
 
@@ -100,16 +101,14 @@
     return mean, inverse
 
 
-def term_kernel(core, lat, gain, bias, cot, sel, keep, send, flat, shifted, up, patches, terms):
+def term_kernel(core, lat, gain, bias, cot, sel, keep, send, flat, shifted, patches, terms):
     clear_edges(shifted)
-    flatten(cot, flat)
-    up[...] = flat[...].astype(jnp.bfloat16)
-    flatten(lat, flat)
+    flat[...] = lat[...].astype(jnp.float32)
     activate(flat, gain, bias, shifted)
     build_patches(shifted, patches)
     for t in range(9):
         at = t * CHANS
-        terms[at : at + CHANS, :] = dot(patches[:, at : at + CHANS], up[...], ((0,), (0,)))
+        terms[at : at + CHANS, :] = dot(patches[:, at : at + CHANS], cot[...], ((0,), (0,)))
     mine, other = sel[core[0]], sel[1 - core[0]]
     for z in range(ZS):
         block = jnp.concatenate(
@@ -117,28 +116,32 @@
         )
         high = block.astype(jnp.bfloat16)
         low = (block - high.astype(jnp.float32)).astype(jnp.bfloat16)
-        keep[z] = dot(mine, high) + dot(mine, low)
-        send[z] = dot(other, high).astype(jnp.bfloat16)
+        zh, zl = divmod(z, LOW)
+        kept = dot(mine, high) + dot(mine, low)
+        sent = dot(other, high).astype(jnp.bfloat16)
+        for yl in range(LOW):
+            keep[zl * LOW + yl, zh] = kept[yl * QUAD : (yl + 1) * QUAD]
+            send[zl * LOW + yl, zh] = sent[yl * QUAD : (yl + 1) * QUAD]
 
 
 def layer_kernel(
-    core, lat, gain, bias, cot, held, got, sel, out, grad, flat, shifted, up, patches, weight
+    core, lat, gain, bias, cot, held, got, sel, out, grad, flat, shifted, patches, weight
 ):
     clear_edges(shifted)
-    flatten(cot, up)
-    flatten(lat, flat)
+    flat[...] = lat[...].astype(jnp.float32)
     mean, inverse = activate(flat, gain, bias, shifted)
     build_patches(shifted, patches)
     mine, other = sel[core[0]], sel[1 - core[0]]
     for z in range(ZS):
-        block = dot(mine, held[z], ((0,), (0,))) + dot(other, got[z], ((0,), (0,)))
+        zh, zl = divmod(z, LOW)
+        ours = jnp.concatenate([held[zl * LOW + yl, zh] for yl in range(LOW)])
+        theirs = jnp.concatenate([got[zl * LOW + yl, zh] for yl in range(LOW)])
+        block = dot(mine, ours, ((0,), (0,))) + dot(other, theirs, ((0,), (0,)))
         for i in range(3):
             at = i * 3 * CHANS + z * ZROWS
             weight[at : at + ZROWS, :] = block[i * ZROWS : (i + 1) * ZROWS].astype(jnp.bfloat16)
-    result = dot(patches[...], weight[...]) + flat[...]
-    shifted[TOP : TOP + CELLS, :] = up[...]
-    for h in range(HEIGHT):
-        out[0, h] = result[h * WIDTH : (h + 1) * WIDTH].astype(jnp.bfloat16)
+    out[...] = (dot(patches[...], weight[...]) + flat[...]).astype(jnp.bfloat16)
+    shifted[TOP : TOP + CELLS, :] = cot[...].astype(jnp.float32)
     build_patches(shifted, patches)
     back = jnp.zeros((CELLS, CHANS), jnp.float32)
     for t in range(9):
@@ -152,13 +155,20 @@
     back = back * (gate * (1.0 + normed * (1.0 - gate))) * gain[...]
     first = group_mean(channel_sum(back))[0:1]
     second = group_mean(channel_sum(back * hat))[0:1]
-    result = up[...] + inverse * (back - first - hat * second)
-    for h in range(HEIGHT):
-        grad[0, h] = result[h * WIDTH : (h + 1) * WIDTH].astype(jnp.bfloat16)
+    result = cot[...].astype(jnp.float32) + inverse * (back - first - hat * second)
+    grad[...] = result.astype(jnp.bfloat16)
 
 
 VMEM = functools.partial(pl.BlockSpec, memory_space=pltpu.VMEM)
 SMEM = functools.partial(pl.BlockSpec, memory_space=pltpu.SMEM)
+
+
+def columns_first(maps):
+    return maps.transpose(0, 2, 1, 3).reshape(CELLS, CHANS)
+
+
+def rows_first(cells):
+    return cells.reshape(1, WIDTH, HEIGHT, CHANS).transpose(0, 2, 1, 3)
 
 
 def spread(block, axis):
@@ -169,37 +179,42 @@
 
 def gather_halves(conv_weight):
     taps, rows, chans = conv_weight.shape
-    block = lax.ppermute(conv_weight.reshape(taps * rows, chans), ("core", "xl"), SWAP)
-    block = spread(block, "y").reshape(YS * taps * rows, chans)
-    block = jnp.pad(block, ((0, PACK - YS * taps * rows), (0, 0)))
-    held = spread(block, "z")
-    return held, lax.ppermute(held, "core", ((0, 1), (1, 0)))
-
-
-def reduce_terms(keep, send):
-    got = lax.ppermute(send, "core", ((0, 1), (1, 0)))
+    block = jnp.pad(conv_weight.reshape(taps * rows, chans), ((0, SLOT - taps * rows), (0, 0)))
+    block = lax.ppermute(block, ("core", "xl"), SWAP)
+    block = spread(block, ("zh", "yh")).reshape(PACKED[1:])
+    held = spread(block, ("zl", "yl"))
+    return held, lax.ppermute(held, "core", TRADE)
+
+
+def halve_terms(keep, send):
+    got = lax.ppermute(send, "core", TRADE)
     own = (keep + got.astype(jnp.float32)).astype(jnp.bfloat16)
-    own = lax.all_to_all(own, "z", 0, 0, tiled=True).astype(jnp.float32).sum(0)
-    own = own[: YS * 3 * ROWS].reshape(YS, 3 * ROWS, CHANS).astype(jnp.bfloat16)
-    own = lax.all_to_all(own, "y", 0, 0, tiled=True).astype(jnp.float32).sum(0)
-    own = spread(own, ("xh", "xl")).sum(0)
-    return lax.ppermute(own, ("core", "xl"), SWAP).reshape(3, ROWS, CHANS)
+    own = lax.all_to_all(own, ("zl", "yl"), 0, 0, tiled=True).astype(jnp.float32).sum(0)
+    own = own.reshape(HIGH * HIGH, SLOT, CHANS).astype(jnp.bfloat16)
+    return lax.all_to_all(own, ("zh", "yh"), 0, 0, tiled=True)
+
+
+def finish_terms(parts):
+    own = parts.astype(jnp.float32).sum(0)
+    for bit in (1, 2):
+        own = own + lax.ppermute(own, "xh", [(k, k ^ bit) for k in range(4)])
+    pair = ("core", "xl")
+    own = lax.ppermute(own, pair, NEAR) + lax.ppermute(own, pair, SWAP)
+    return own[: 3 * ROWS].reshape(3, ROWS, CHANS)
 
 
 def terms_of(core, latents, gain, bias, cotangent, sel, **options):
-    packed = (ZS, PACK, CHANS)
     return pl.pallas_call(
         term_kernel,
         out_shape=(
-            jax.ShapeDtypeStruct(packed, jnp.float32),
-            jax.ShapeDtypeStruct(packed, jnp.bfloat16),
+            jax.ShapeDtypeStruct(PACKED, jnp.float32),
+            jax.ShapeDtypeStruct(PACKED, jnp.bfloat16),
         ),
         in_specs=[SMEM()] + [VMEM()] * 5,
         out_specs=(VMEM(), VMEM()),
         scratch_shapes=[
             pltpu.VMEM((CELLS, CHANS), jnp.float32),
             pltpu.VMEM((CELLS + 2 * TOP, CHANS), jnp.float32),
-            pltpu.VMEM((CELLS, CHANS), jnp.bfloat16),
             pltpu.VMEM((CELLS, 9 * CHANS), jnp.bfloat16),
             pltpu.VMEM((9 * CHANS, CHANS), jnp.float32),
         ],
@@ -223,7 +238,6 @@
         scratch_shapes=[
             pltpu.VMEM((CELLS, CHANS), jnp.float32),
             pltpu.VMEM((CELLS + 2 * TOP, CHANS), jnp.float32),
-            pltpu.VMEM((CELLS, CHANS), jnp.float32),
             pltpu.VMEM((CELLS, 9 * CHANS), jnp.bfloat16),
             pltpu.VMEM((9 * CHANS, CHANS), jnp.bfloat16),
         ],
@@ -241,16 +255,19 @@
     gain, bias = norm_gain[None], norm_bias[None]
     sel = jnp.asarray(SEL, jnp.bfloat16)
     held, got = gather_halves(conv_weight)
+    latents, cotangent = columns_first(latents), columns_first(cotangent)
     keep, send = terms_of(core, latents, gain, bias, cotangent, sel)
-    grad_weight = reduce_terms(keep, send) * scale
+    parts = halve_terms(keep, send)
     output, grad_input = layer_of(core, latents, gain, bias, cotangent, held, got, sel)
-    return (output, grad_input, grad_weight)
+    parts, output, grad_input = lax.optimization_barrier((parts, output, grad_input))
+    grad_weight = finish_terms(parts) * scale
+    return (rows_first(output), rows_first(grad_input), grad_weight)
 
 
 def solution(mesh):
-    fine = Mesh(mesh.devices.reshape(4, 2, 8, 2, 8), AXES)
-    batch = P(("xh", "core", "z", "xl", "y"), None, None, None)
-    weight = P(None, ("z", "xl", "y"), None)
+    fine = Mesh(mesh.devices.reshape(4, 2, HIGH, LOW, 2, HIGH, LOW), AXES)
+    batch = P(AXES, None, None, None)
+    weight = P(None, ("zh", "zl", "xl", "yh", "yl"), None)
     return jax.shard_map(
         body,
         mesh=fine,

time: 168 us -> 139 us (0.83)
  blocking collectives: 45.8 us -> 0 us
  starting transfers between devices: 35.9 us -> 63 us
  waiting for transfers between devices: 58.7 us -> 45 us
  other arithmetic: 3.03 us -> 4.84 us
    all_to_all x3 -> x0, blocking collectives: 45.8 us -> none  [the longest x2 33.7 us: spread(): return lax.all_to_all(copies, axis, 0, 0, tiled=True)]
    all_to_all x1 -> x2, waiting for transfers between devices: 33.9 us -> 19.1 us  [the longest x1 15.5 us: halve_terms(): lax.all_to_all(own, ('zl', 'yl'), 0, 0, tiled=True).astype(jnp.float32)]
    ppermute x4 -> x7, starting transfers between devices: 15.1 us -> 28.6 us  [the longest x2 11.2 us: finish_terms(): own = own + lax.ppermute(own, 'xh', [(k, k ^ bit) for k in range(4)])]
    all_to_all x1 -> x2, starting transfers between devices: 16.5 us -> 25 us  [spread(): return lax.all_to_all(copies, axis, 0, 0, tiled=True)]
    all_to_all x1 -> x2, starting transfers between devices: 4.26 us -> 9.38 us  [the longest x1 5.07 us: halve_terms(): return lax.all_to_all(own, ('zh', 'yh'), 0, 0, tiled=True)]
    ppermute x4 -> x7, waiting for transfers between devices: 4.6 us -> 9.06 us  [the longest x2 3.28 us: finish_terms(): own = own + lax.ppermute(own, 'xh', [(k, k ^ bit) for k in range(4)])]
    all_to_all x1 -> x2, waiting for transfers between devices: 20.2 us -> 16.8 us  [spread(): return lax.all_to_all(copies, axis, 0, 0, tiled=True)]
    reduce_sum x3 -> x2, other arithmetic: 1.6 us -> 3.43 us  [the longest x1 2.36 us: halve_terms(): lax.all_to_all(own, ('zl', 'yl'), 0, 0, tiled=True).astype(jnp.float32)]
  transfers between devices with their start and end apart: 6 -> 11, of which waited for: 4 -> 9; matrix products, arithmetic and copies ran while one was open for 3% -> 4% of each run, Pallas kernels for 11% -> 12%
where the time goes in v3:
time: 139 us; the launch traced here: 137 us
  starting transfers between devices  63 us (45%)
  waiting for transfers between devices  45 us (32%)
  Pallas kernels  16.5 us (12%)
  local copies, waits for them, and re-layouts  6.33 us (5%)
  other arithmetic  4.84 us (3%)
    all_to_all x2, starting transfers between devices, spread(): return lax.all_to_all(copies, axis, 0, 0, tiled=True)  25 us
    all_to_all x2, waiting for transfers between devices, spread(): return lax.all_to_all(copies, axis, 0, 0, tiled=True)  16.8 us
    all_to_all x1, waiting for transfers between devices, halve_terms(): lax.all_to_all(own, ('zl', 'yl'), 0, 0, tiled=True).astype(jnp.float32)  15.5 us
    ppermute x2, starting transfers between devices, finish_terms(): own = own + lax.ppermute(own, 'xh', [(k, k ^ bit) for k in range(4)])  11.2 us
    pallas_call x1, Pallas kernels, layer_of(): pl.pallas_call(layer_kernel, out_shape=(jax.ShapeDtypeStruct(latents.shap...  9.64 us
    ppermute x2, starting transfers between devices, finish_terms(): own = lax.ppermute(own, pair, NEAR) + lax.ppermute(own, pair, SWAP)  9.02 us
    pallas_call x1, Pallas kernels, terms_of(): pl.pallas_call(term_kernel, out_shape=(jax.ShapeDtypeStruct(PACKED, jnp.f...  6.9 us
    all_to_all x1, starting transfers between devices, halve_terms(): return lax.all_to_all(own, ('zh', 'yh'), 0, 0, tiled=True)  5.07 us
  transfers between devices with their start and end apart: 11, of which 9 were waited for; matrix products, arithmetic and copies ran while one was open for 4% of the time, Pallas kernels for 12%

profile of v3, /device:TPU:1, one launch (start us, length us, event | category | flops | bytes accessed | tf_op | source)
XLA Modules:
  0.0 136.5 jit_solution(239105181130621020)
XLA Ops:
  1.4 4.5 %collective-permute-start.1 = (bf16[28,384]{1,0:T(8,128)(2,1)S(1)}, bf16[28,384]{1,0:T(8,128)(2,1)S(1)}, u32[]{:S(2)}, u32[]{:S(2)}) collective-permute-start(bf16[28,384]{1,0:T(8,128)(2,1)S(1)} %pad.4), channel_id=1, source_target_pairs={{0,0},{8,128},{128,8},{136,136},{1,1},{9,129},{129,9},{137,137},{2... | collective-permute-start | bytes 64520 | tf_op jit(solution)/shard_map/ppermute | solution.py:183
  6.0 1.5 %collective-permute-done.1 = bf16[28,384]{1,0:T(8,128)(2,1)S(1)} collective-permute-done((bf16[28,384]{1,0:T(8,128)(2,1)S(1)}, bf16[28,384]{1,0:T(8,128)(2,1)S(1)}, u32[]{:S(2)}, u32[]{:S(2)}) %collective-permute-start.1) | collective-permute-done | bytes 21536 | tf_op jit(solution)/shard_map/ppermute | solution.py:183
  8.2 21.3 %all-to-all-start.2 = ((bf16[16,28,384]{2,1,0:T(8,128)(2,1)}), bf16[16,28,384]{2,1,0:T(8,128)(2,1)S(1)}, u32[]{:S(2)}, u32[]{:S(2)}) async-start(bf16[16,28,384]{2,1,0:T(8,128)(2,1)} %broadcast_in_dim.21), calls=%async_computation.2 | async-start | bytes 786432 | tf_op jit(solution)/shard_map/all_to_all | solution.py:177
  29.6 14.0 %all-to-all-done.2 = bf16[16,28,384]{2,1,0:T(8,128)(2,1)S(1)} async-done(((bf16[16,28,384]{2,1,0:T(8,128)(2,1)}), bf16[16,28,384]{2,1,0:T(8,128)(2,1)S(1)}, u32[]{:S(2)}, u32[]{:S(2)}) %all-to-all-start.2) | async-done | bytes 344096 | tf_op jit(solution)/shard_map/all_to_all | solution.py:177
  44.9 3.7 %all-to-all-start.3 = ((bf16[4,4,112,384]{3,2,1,0:T(8,128)(2,1)}), bf16[4,4,112,384]{3,2,1,0:T(8,128)(2,1)S(1)}, u32[]{:S(2)}, u32[]{:S(2)}) async-start(bf16[4,4,112,384]{3,2,1,0:T(8,128)(2,1)} %broadcast_in_dim.23), calls=%async_computation.3 | async-start | bytes 2752512 | tf_op jit(solution)/shard_map/all_to_all | solution.py:177
  48.6 6.9 %shard_map.85 = (f32[4,4,112,384]{3,2,1,0:T(8,128)S(1)}, bf16[4,4,112,384]{3,2,1,0:T(8,128)(2,1)S(1)}) custom-call(s32[1]{0:T(128)} %bitcast.core, bf16[480,384]{1,0:T(8,128)(2,1)S(1)} %bitcast.13, f32[1,384]{1,0:T(1,128)S(1)} %broadcast_in_dim.19.gain, f32[1,384]{1,0:T(1,128)S(1)} %broadcast_in_dim.20.bias, bf16[480,384]{1,0:T(8,128)(2,1)S(1)} %bitcast.15, ...), custom_call_target="tpu_custom_call" | custom-call | flops 4000000000 | bytes 8000000 | tf_op jit(solution)/shard_map/pallas_call | solution.py:207
  55.5 1.9 %collective-permute-start = (bf16[4,4,112,384]{3,2,1,0:T(8,128)(2,1)S(1)}, bf16[4,4,112,384]{3,2,1,0:T(8,128)(2,1)S(1)}, u32[]{:S(2)}, u32[]{:S(2)}) collective-permute-start(bf16[4,4,112,384]{3,2,1,0:T(8,128)(2,1)S(1)} %get-tuple-element.11), channel_id=1, source_target_pairs={{0,128},{128,0},{1,129},{129,1},{2,130},{130,2},{3,131},{131,3},{4... | collective-permute-start | bytes 4128776 | tf_op jit(solution)/shard_map/ppermute | solution.py:190
  57.4 3.1 %collective-permute-done = bf16[4,4,112,384]{3,2,1,0:T(8,128)(2,1)S(1)} collective-permute-done((bf16[4,4,112,384]{3,2,1,0:T(8,128)(2,1)S(1)}, bf16[4,4,112,384]{3,2,1,0:T(8,128)(2,1)S(1)}, u32[]{:S(2)}, u32[]{:S(2)}) %collective-permute-start) | collective-permute-done | bytes 1376288 | tf_op jit(solution)/shard_map/ppermute | solution.py:190
  60.5 1.4 %add_convert_fusion = bf16[4,4,112,384]{3,2,1,0:T(8,128)(2,1)} fusion(f32[4,4,112,384]{3,2,1,0:T(8,128)S(1)} %get-tuple-element.10, bf16[4,4,112,384]{3,2,1,0:T(8,128)(2,1)S(1)} %collective-permute-done), kind=kLoop, calls=%fused_computation | loop fusion | flops 2064384 | bytes 5505024 | tf_op jit(solution)/shard_map/convert_element_type | solution.py:191
  61.9 2.8 %all-to-all-done.3.held = bf16[4,4,112,384]{3,2,1,0:T(8,128)(2,1)S(1)} async-done(((bf16[4,4,112,384]{3,2,1,0:T(8,128)(2,1)}), bf16[4,4,112,384]{3,2,1,0:T(8,128)(2,1)S(1)}, u32[]{:S(2)}, u32[]{:S(2)}) %all-to-all-start.3) | async-done | bytes 1376288 | tf_op jit(solution)/shard_map/all_to_all | solution.py:177
  64.8 4.3 %all-to-all-start = ((bf16[4,4,112,384]{3,2,1,0:T(8,128)(2,1)}), bf16[4,4,112,384]{3,2,1,0:T(8,128)(2,1)}, u32[]{:S(2)}, u32[]{:S(2)}) async-start(bf16[4,4,112,384]{3,2,1,0:T(8,128)(2,1)} %add_convert_fusion), calls=%async_computation | async-start | bytes 2752512 | tf_op jit(solution)/shard_map/all_to_all | solution.py:192
  69.1 1.9 %collective-permute-start.2 = (bf16[4,4,112,384]{3,2,1,0:T(8,128)(2,1)S(1)}, bf16[4,4,112,384]{3,2,1,0:T(8,128)(2,1)S(1)}, u32[]{:S(2)}, u32[]{:S(2)}) collective-permute-start(bf16[4,4,112,384]{3,2,1,0:T(8,128)(2,1)S(1)} %all-to-all-done.3.held), channel_id=1, source_target_pairs={{0,128},{128,0},{1,129},{129,1},{2,130},{130,2},{3,131},{131,3},{4... | collective-permute-start | bytes 4128776 | tf_op jit(solution)/shard_map/ppermute | solution.py:186
  71.0 15.5 %all-to-all-done = bf16[4,4,112,384]{3,2,1,0:T(8,128)(2,1)} async-done(((bf16[4,4,112,384]{3,2,1,0:T(8,128)(2,1)}), bf16[4,4,112,384]{3,2,1,0:T(8,128)(2,1)}, u32[]{:S(2)}, u32[]{:S(2)}) %all-to-all-start) | async-done | bytes 1376288 | tf_op jit(solution)/shard_map/all_to_all | solution.py:192
  86.5 2.4 %reduce_sum.21 = bf16[4,112,384]{2,1,0:T(8,128)(2,1)} reduce(bf16[4,4,112,384]{3,2,1,0:T(8,128)(2,1)} %all-to-all-done, bf16[]{:T(256)} %constant.13.clone.1), dimensions={0}, to_apply=%region_0.1 | reduce | flops 516096 | bytes 1720322 | tf_op jit(solution)/shard_map/reduce_sum | solution.py:192
  88.9 1.8 %convert_element_type.18 = bf16[16,28,384]{2,1,0:T(8,128)(2,1)} reshape(bf16[4,112,384]{2,1,0:T(8,128)(2,1)} %reduce_sum.21) | data formatting | bytes 688128 | tf_op jit(solution)/shard_map/convert_element_type | solution.py:193
  90.7 5.1 %all-to-all-start.1 = ((bf16[16,28,384]{2,1,0:T(8,128)(2,1)}), bf16[16,28,384]{2,1,0:T(8,128)(2,1)}, u32[]{:S(2)}, u32[]{:S(2)}) async-start(bf16[16,28,384]{2,1,0:T(8,128)(2,1)} %convert_element_type.18), calls=%async_computation.1 | async-start | bytes 786432 | tf_op jit(solution)/shard_map/all_to_all | solution.py:194
  96.8 9.6 %shard_map.86 = (bf16[480,384]{1,0:T(8,128)(2,1)}, bf16[480,384]{1,0:T(8,128)(2,1)}) custom-call(s32[1]{0:T(128)} %bitcast.core, bf16[480,384]{1,0:T(8,128)(2,1)S(1)} %bitcast.14, f32[1,384]{1,0:T(1,128)S(1)} %broadcast_in_dim.19.gain, f32[1,384]{1,0:T(1,128)S(1)} %broadcast_in_dim.20.bias, bf16[480,384]{1,0:T(8,128)(2,1)S(1)} %bitcast.16, ...), custom_call_target="tpu_custom_call" | custom-call | flops 4000000000 | bytes 8000000 | tf_op jit(solution)/shard_map/pallas_call | solution.py:230
  106.4 3.6 %all-to-all-done.1 = bf16[16,28,384]{2,1,0:T(8,128)(2,1)} async-done(((bf16[16,28,384]{2,1,0:T(8,128)(2,1)}), bf16[16,28,384]{2,1,0:T(8,128)(2,1)}, u32[]{:S(2)}, u32[]{:S(2)}) %all-to-all-start.1) | async-done | bytes 344096 | tf_op jit(solution)/shard_map/all_to_all | solution.py:194
  111.1 4.0 %collective-permute-start.3 = (f32[28,384]{1,0:T(8,128)S(1)}, f32[28,384]{1,0:T(8,128)S(1)}, u32[]{:S(2)}, u32[]{:S(2)}) collective-permute-start(f32[28,384]{1,0:T(8,128)S(1)} %convert_reduce_fusion), channel_id=1, source_target_pairs={{0,256},{256,0},{512,768},{768,512},{1,257},{257,1},{513,769},{769... | collective-permute-start | bytes 129032 | tf_op jit(solution)/shard_map/ppermute | solution.py:200
  115.1 1.7 %collective-permute-done.3 = f32[28,384]{1,0:T(8,128)S(1)} collective-permute-done((f32[28,384]{1,0:T(8,128)S(1)}, f32[28,384]{1,0:T(8,128)S(1)}, u32[]{:S(2)}, u32[]{:S(2)}) %collective-permute-start.3) | collective-permute-done | bytes 43040 | tf_op jit(solution)/shard_map/ppermute | solution.py:200
  116.8 7.2 %collective-permute-start.4 = (f32[28,384]{1,0:T(8,128)S(1)}, f32[28,384]{1,0:T(8,128)S(1)}, u32[]{:S(2)}, u32[]{:S(2)}) collective-permute-start(f32[28,384]{1,0:T(8,128)S(1)} %add.15), channel_id=1, source_target_pairs={{0,512},{256,768},{512,0},{768,256},{1,513},{257,769},{513,1},{769... | collective-permute-start | bytes 129032 | tf_op jit(solution)/shard_map/ppermute | solution.py:200
  124.0 1.6 %collective-permute-done.4 = f32[28,384]{1,0:T(8,128)S(1)} collective-permute-done((f32[28,384]{1,0:T(8,128)S(1)}, f32[28,384]{1,0:T(8,128)S(1)}, u32[]{:S(2)}, u32[]{:S(2)}) %collective-permute-start.4) | collective-permute-done | bytes 43040 | tf_op jit(solution)/shard_map/ppermute | solution.py:200
  125.6 7.1 %collective-permute-start.6 = (f32[28,384]{1,0:T(8,128)S(1)}, f32[28,384]{1,0:T(8,128)S(1)}, u32[]{:S(2)}, u32[]{:S(2)}) collective-permute-start(f32[28,384]{1,0:T(8,128)S(1)} %add.16), channel_id=1, source_target_pairs={{0,0},{8,128},{128,8},{136,136},{1,1},{9,129},{129,9},{137,137},{2... | collective-permute-start | bytes 129032 | tf_op jit(solution)/shard_map/ppermute | solution.py:202
  132.7 1.9 %collective-permute-start.5 = (f32[28,384]{1,0:T(8,128)S(1)}, f32[28,384]{1,0:T(8,128)S(1)}, u32[]{:S(2)}, u32[]{:S(2)}) collective-permute-start(f32[28,384]{1,0:T(8,128)S(1)} %add.16), channel_id=1, source_target_pairs={{8,0},{128,136},{136,8},{0,128},{9,1},{129,137},{137,9},{1,129},{1... | collective-permute-start | bytes 129032 | tf_op jit(solution)/shard_map/ppermute | solution.py:202
  (29 shorter events, 6.8 us)
Async XLA Ops:
  0.6 28.9 %copy-start.4 = (f32[384]{0:T(512)S(1)}, f32[384]{0:T(512)}, u32[]{:S(2)}) copy-start(f32[384]{0:T(512)} %param.7) | copy-start | bytes 4612
  0.6 28.9 %copy-start.5 = (f32[384]{0:T(512)S(1)}, f32[384]{0:T(512)}, u32[]{:S(2)}) copy-start(f32[384]{0:T(512)} %param.8) | copy-start | bytes 4612
  1.4 6.0 %collective-permute-start.1 = (bf16[28,384]{1,0:T(8,128)(2,1)S(1)}, bf16[28,384]{1,0:T(8,128)(2,1)S(1)}, u32[]{:S(2)}, u32[]{:S(2)}) collective-permute-start(bf16[28,384]{1,0:T(8,128)(2,1)S(1)} %pad.4), channel_id=1, source_target_pairs={{0,0},{8,128},{128,8},{136,136},{1,1},{9,129},{129,9},{137,137},{2... | collective-permute-start | bytes 64520 | tf_op jit(solution)/shard_map/ppermute | solution.py:183
  8.2 35.4 %all-to-all-start.2 = ((bf16[16,28,384]{2,1,0:T(8,128)(2,1)}), bf16[16,28,384]{2,1,0:T(8,128)(2,1)S(1)}, u32[]{:S(2)}, u32[]{:S(2)}) async-start(bf16[16,28,384]{2,1,0:T(8,128)(2,1)} %broadcast_in_dim.21), calls=%async_computation.2 | async-start | bytes 786432 | tf_op jit(solution)/shard_map/all_to_all | solution.py:177
  44.9 3.7 %copy-start = (bf16[1,24,20,384]{3,1,2,0:T(8,128)(2,1)S(1)}, bf16[1,24,20,384]{3,1,2,0:T(8,128)(2,1)}, u32[]{:S(2)}) copy-start(bf16[1,24,20,384]{3,1,2,0:T(8,128)(2,1)} %param.6) | copy-start | bytes 1105924
  44.9 3.7 %copy-start.1 = (bf16[1,24,20,384]{3,1,2,0:T(8,128)(2,1)S(1)}, bf16[1,24,20,384]{3,1,2,0:T(8,128)(2,1)}, u32[]{:S(2)}) copy-start(bf16[1,24,20,384]{3,1,2,0:T(8,128)(2,1)} %param.10) | copy-start | bytes 1105924
  44.9 3.7 %copy-start.2 = (bf16[2,224,432]{2,1,0:T(8,128)(2,1)S(1)}, bf16[2,224,432]{2,1,0:T(8,128)(2,1)}, u32[]{:S(2)}) copy-start(bf16[2,224,432]{2,1,0:T(8,128)(2,1)} %constant.16.clone.sel) | copy-start | bytes 1161220
  44.9 19.9 %all-to-all-start.3 = ((bf16[4,4,112,384]{3,2,1,0:T(8,128)(2,1)}), bf16[4,4,112,384]{3,2,1,0:T(8,128)(2,1)S(1)}, u32[]{:S(2)}, u32[]{:S(2)}) async-start(bf16[4,4,112,384]{3,2,1,0:T(8,128)(2,1)} %broadcast_in_dim.23), calls=%async_computation.3 | async-start | bytes 2752512 | tf_op jit(solution)/shard_map/all_to_all | solution.py:177
  55.5 5.0 %collective-permute-start = (bf16[4,4,112,384]{3,2,1,0:T(8,128)(2,1)S(1)}, bf16[4,4,112,384]{3,2,1,0:T(8,128)(2,1)S(1)}, u32[]{:S(2)}, u32[]{:S(2)}) collective-permute-start(bf16[4,4,112,384]{3,2,1,0:T(8,128)(2,1)S(1)} %get-tuple-element.11), channel_id=1, source_target_pairs={{0,128},{128,0},{1,129},{129,1},{2,130},{130,2},{3,131},{131,3},{4... | collective-permute-start | bytes 4128776 | tf_op jit(solution)/shard_map/ppermute | solution.py:190
  64.8 21.8 %all-to-all-start = ((bf16[4,4,112,384]{3,2,1,0:T(8,128)(2,1)}), bf16[4,4,112,384]{3,2,1,0:T(8,128)(2,1)}, u32[]{:S(2)}, u32[]{:S(2)}) async-start(bf16[4,4,112,384]{3,2,1,0:T(8,128)(2,1)} %add_convert_fusion), calls=%async_computation | async-start | bytes 2752512 | tf_op jit(solution)/shard_map/all_to_all | solution.py:192
  69.1 26.7 %collective-permute-start.2 = (bf16[4,4,112,384]{3,2,1,0:T(8,128)(2,1)S(1)}, bf16[4,4,112,384]{3,2,1,0:T(8,128)(2,1)S(1)}, u32[]{:S(2)}, u32[]{:S(2)}) collective-permute-start(bf16[4,4,112,384]{3,2,1,0:T(8,128)(2,1)S(1)} %all-to-all-done.3.held), channel_id=1, source_target_pairs={{0,128},{128,0},{1,129},{129,1},{2,130},{130,2},{3,131},{131,3},{4... | collective-permute-start | bytes 4128776 | tf_op jit(solution)/shard_map/ppermute | solution.py:186
  90.7 19.3 %all-to-all-start.1 = ((bf16[16,28,384]{2,1,0:T(8,128)(2,1)}), bf16[16,28,384]{2,1,0:T(8,128)(2,1)}, u32[]{:S(2)}, u32[]{:S(2)}) async-start(bf16[16,28,384]{2,1,0:T(8,128)(2,1)} %convert_element_type.18), calls=%async_computation.1 | async-start | bytes 786432 | tf_op jit(solution)/shard_map/all_to_all | solution.py:194
  95.8 1.0 copy-start.3
  111.1 5.7 %collective-permute-start.3 = (f32[28,384]{1,0:T(8,128)S(1)}, f32[28,384]{1,0:T(8,128)S(1)}, u32[]{:S(2)}, u32[]{:S(2)}) collective-permute-start(f32[28,384]{1,0:T(8,128)S(1)} %convert_reduce_fusion), channel_id=1, source_target_pairs={{0,256},{256,0},{512,768},{768,512},{1,257},{257,1},{513,769},{769... | collective-permute-start | bytes 129032 | tf_op jit(solution)/shard_map/ppermute | solution.py:200
  116.8 8.8 %collective-permute-start.4 = (f32[28,384]{1,0:T(8,128)S(1)}, f32[28,384]{1,0:T(8,128)S(1)}, u32[]{:S(2)}, u32[]{:S(2)}) collective-permute-start(f32[28,384]{1,0:T(8,128)S(1)} %add.15), channel_id=1, source_target_pairs={{0,512},{256,768},{512,0},{768,256},{1,513},{257,769},{513,1},{769... | collective-permute-start | bytes 129032 | tf_op jit(solution)/shard_map/ppermute | solution.py:200
  125.6 9.0 %collective-permute-start.6 = (f32[28,384]{1,0:T(8,128)S(1)}, f32[28,384]{1,0:T(8,128)S(1)}, u32[]{:S(2)}, u32[]{:S(2)}) collective-permute-start(f32[28,384]{1,0:T(8,128)S(1)} %add.16), channel_id=1, source_target_pairs={{0,0},{8,128},{128,8},{136,136},{1,1},{9,129},{129,9},{137,137},{2... | collective-permute-start | bytes 129032 | tf_op jit(solution)/shard_map/ppermute | solution.py:202
  132.7 3.1 %collective-permute-start.5 = (f32[28,384]{1,0:T(8,128)S(1)}, f32[28,384]{1,0:T(8,128)S(1)}, u32[]{:S(2)}, u32[]{:S(2)}) collective-permute-start(f32[28,384]{1,0:T(8,128)S(1)} %add.16), channel_id=1, source_target_pairs={{8,0},{128,136},{136,8},{0,128},{9,1},{129,137},{137,9},{1,129},{1... | collective-permute-start | bytes 129032 | tf_op jit(solution)/shard_map/ppermute | solution.py:202

commit v4 on v3

--- a/solution.py
+++ b/solution.py
@@ -101,7 +101,7 @@
     return mean, inverse
 
 
-def term_kernel(core, lat, gain, bias, cot, sel, keep, send, flat, shifted, patches, terms):
+def term_kernel(here, lat, gain, bias, cot, sel, keep, send, flat, shifted, patches, terms):
     clear_edges(shifted)
     flat[...] = lat[...].astype(jnp.float32)
     activate(flat, gain, bias, shifted)
@@ -109,7 +109,7 @@
     for t in range(9):
         at = t * CHANS
         terms[at : at + CHANS, :] = dot(patches[:, at : at + CHANS], cot[...], ((0,), (0,)))
-    mine, other = sel[core[0]], sel[1 - core[0]]
+    mine, other = sel[here[0]], sel[1 - here[0]]
     for z in range(ZS):
         block = jnp.concatenate(
             [terms[i * 3 * CHANS + z * ZROWS : i * 3 * CHANS + (z + 1) * ZROWS, :] for i in range(3)]
@@ -125,17 +125,19 @@
 
 
 def layer_kernel(
-    core, lat, gain, bias, cot, held, got, sel, out, grad, flat, shifted, patches, weight
+    here, lat, gain, bias, cot, held, got, sel, out, grad, flat, shifted, patches, weight
 ):
     clear_edges(shifted)
     flat[...] = lat[...].astype(jnp.float32)
     mean, inverse = activate(flat, gain, bias, shifted)
     build_patches(shifted, patches)
-    mine, other = sel[core[0]], sel[1 - core[0]]
+    mine, other = sel[here[0]], sel[1 - here[0]]
     for z in range(ZS):
         zh, zl = divmod(z, LOW)
-        ours = jnp.concatenate([held[zl * LOW + yl, zh] for yl in range(LOW)])
-        theirs = jnp.concatenate([got[zl * LOW + yl, zh] for yl in range(LOW)])
+        ahead = lax.rem(zh + HIGH - here[1], HIGH)
+        flips = [(zl ^ here[2]) * LOW + (yl ^ here[3]) for yl in range(LOW)]
+        ours = jnp.concatenate([held[flip, ahead] for flip in flips])
+        theirs = jnp.concatenate([got[flip, ahead] for flip in flips])
         block = dot(mine, ours, ((0,), (0,))) + dot(other, theirs, ((0,), (0,)))
         for i in range(3):
             at = i * 3 * CHANS + z * ZROWS
@@ -171,39 +173,53 @@
     return cells.reshape(1, WIDTH, HEIGHT, CHANS).transpose(0, 2, 1, 3)
 
 
-def spread(block, axis):
-    count = lax.axis_size(axis)
-    copies = jnp.broadcast_to(block[None], (count,) + block.shape)
-    return lax.all_to_all(copies, axis, 0, 0, tiled=True)
-
-
-def gather_halves(conv_weight):
+def gather_slots(conv_weight):
     taps, rows, chans = conv_weight.shape
     block = jnp.pad(conv_weight.reshape(taps * rows, chans), ((0, SLOT - taps * rows), (0, 0)))
-    block = lax.ppermute(block, ("core", "xl"), SWAP)
-    block = spread(block, ("zh", "yh")).reshape(PACKED[1:])
-    held = spread(block, ("zl", "yl"))
-    return held, lax.ppermute(held, "core", TRADE)
-
-
-def halve_terms(keep, send):
+    slots = [lax.ppermute(block, ("core", "xl", "yh"), from_ahead(j)) for j in range(HIGH)]
+    ahead = lax.rem(HIGH - lax.axis_index("yh"), HIGH)
+    return lax.dynamic_slice_in_dim(jnp.stack(slots + slots[:-1]), ahead, HIGH).reshape(QUAD, chans)
+
+
+def gather_half(block):
+    ring = range(HIGH)
+    steps = [[((k + j) % HIGH, k) for k in ring] for j in ring[1:]]
+    block = jnp.stack([block] + [lax.ppermute(block, "zh", step) for step in steps])
+    flips = [[(k ^ bits, k) for k in range(4)] for bits in (1, 2, 3)]
+    return jnp.stack([block] + [lax.ppermute(block, ("zl", "yl"), flip) for flip in flips])
+
+
+def from_ahead(j):
+    return [
+        ((x * 2 + c) * HIGH + (y + j) % HIGH, (c * 2 + x) * HIGH + y)
+        for c in range(2)
+        for y in range(HIGH)
+        for x in range(2)
+    ]
+
+
+def add_cores(keep, send):
     got = lax.ppermute(send, "core", TRADE)
-    own = (keep + got.astype(jnp.float32)).astype(jnp.bfloat16)
+    return (keep + got.astype(jnp.float32)).astype(jnp.bfloat16)
+
+
+def add_neighbours(own):
     own = lax.all_to_all(own, ("zl", "yl"), 0, 0, tiled=True).astype(jnp.float32).sum(0)
-    own = own.reshape(HIGH * HIGH, SLOT, CHANS).astype(jnp.bfloat16)
-    return lax.all_to_all(own, ("zh", "yh"), 0, 0, tiled=True)
+    return own.reshape(HIGH * HIGH, SLOT, CHANS).astype(jnp.bfloat16)
 
 
 def finish_terms(parts):
     own = parts.astype(jnp.float32).sum(0)
-    for bit in (1, 2):
-        own = own + lax.ppermute(own, "xh", [(k, k ^ bit) for k in range(4)])
+    near, far, both = [
+        lax.ppermute(own, "xh", [(k, k ^ bits) for k in range(4)]) for bits in (1, 2, 3)
+    ]
+    own = (own + far) + (near + both)
     pair = ("core", "xl")
     own = lax.ppermute(own, pair, NEAR) + lax.ppermute(own, pair, SWAP)
     return own[: 3 * ROWS].reshape(3, ROWS, CHANS)
 
 
-def terms_of(core, latents, gain, bias, cotangent, sel, **options):
+def terms_of(here, latents, gain, bias, cotangent, sel, **options):
     return pl.pallas_call(
         term_kernel,
         out_shape=(
@@ -223,10 +239,10 @@
             flops=4 * 10**9, bytes_accessed=8 * 10**6, transcendentals=CELLS * CHANS
         ),
         **options,
-    )(core, latents, gain, bias, cotangent, sel)
-
-
-def layer_of(core, latents, gain, bias, cotangent, held, got, sel, **options):
+    )(here, latents, gain, bias, cotangent, sel)
+
+
+def layer_of(here, latents, gain, bias, cotangent, held, got, sel, **options):
     return pl.pallas_call(
         layer_kernel,
         out_shape=(
@@ -246,19 +262,22 @@
             flops=4 * 10**9, bytes_accessed=8 * 10**6, transcendentals=2 * CELLS * CHANS
         ),
         **options,
-    )(core, latents, gain, bias, cotangent, held, got, sel)
+    )(here, latents, gain, bias, cotangent, held, got, sel)
 
 
 def body(latents, norm_gain, norm_bias, conv_weight, cotangent):
     scale = 1.0 / (latents.shape[0] * lax.axis_size(AXES))
-    core = lax.axis_index("core").reshape(1)
+    here = jnp.stack([lax.axis_index(axis) for axis in ("core", "zh", "zl", "yl")])
     gain, bias = norm_gain[None], norm_bias[None]
     sel = jnp.asarray(SEL, jnp.bfloat16)
-    held, got = gather_halves(conv_weight)
     latents, cotangent = columns_first(latents), columns_first(cotangent)
-    keep, send = terms_of(core, latents, gain, bias, cotangent, sel)
-    parts = halve_terms(keep, send)
-    output, grad_input = layer_of(core, latents, gain, bias, cotangent, held, got, sel)
+    keep, send = terms_of(here, latents, gain, bias, cotangent, sel)
+    keep, send, conv_weight = lax.optimization_barrier((keep, send, conv_weight))
+    own, block = lax.optimization_barrier((add_cores(keep, send), gather_slots(conv_weight)))
+    own, held = lax.optimization_barrier((add_neighbours(own), gather_half(block)))
+    parts = lax.all_to_all(own, ("zh", "yh"), 0, 0, tiled=True)
+    got = lax.ppermute(held, "core", TRADE)
+    output, grad_input = layer_of(here, latents, gain, bias, cotangent, held, got, sel)
     parts, output, grad_input = lax.optimization_barrier((parts, output, grad_input))
     grad_weight = finish_terms(parts) * scale
     return (rows_first(output), rows_first(grad_input), grad_weight)

time: 139 us -> 161 us (1.16)
  starting transfers between devices: 63 us -> 86.6 us
  waiting for transfers between devices: 45 us -> 39.9 us
  local copies, waits for them, and re-layouts: 6.33 us -> 9.06 us
    ppermute x5 -> x15, starting transfers between devices: 19.6 us -> 66.3 us  [the longest x4 19.5 us: gather_slots(): lax.ppermute(block, ('core', 'xl', 'yh'), from_ahead(j))]
    all_to_all x4 -> x2, waiting for transfers between devices: 35.9 us -> 3.63 us  [the longest x1 3.63 us: body(): parts = lax.all_to_all(own, ('zh', 'yh'), 0, 0, tiled=True)]
    ppermute x5 -> x15, waiting for transfers between devices: 7.87 us -> 35.1 us  [the longest x3 13.3 us: gather_half(): lax.ppermute(block, 'zh', step)]
    all_to_all x4 -> x2, starting transfers between devices: 34.4 us -> 12.1 us  [the longest x1 8.52 us: body(): parts = lax.all_to_all(own, ('zh', 'yh'), 0, 0, tiled=True)]
    unnamed x14 -> x23, local copies, waits for them, and re-layouts: 2.44 us -> 5.82 us
    broadcast_in_dim x3 -> x0, local copies, waits for them, and re-layouts: 2.06 us -> none  [spread(): copies = jnp.broadcast_to(block[None], (count,) + block.shape)]
  transfers between devices with their start and end apart: 11 -> 19, of which waited for: 9 -> 8; matrix products, arithmetic and copies ran while one was open for 4% -> 0% of each run, Pallas kernels for 12% -> 6%
where the time goes in v4:
time: 161 us; the launch traced here: 160 us
  starting transfers between devices  86.6 us (54%)
  waiting for transfers between devices  39.9 us (25%)
  Pallas kernels  17.8 us (11%)
  local copies, waits for them, and re-layouts  9.06 us (6%)
  other arithmetic  5.28 us (3%)
    ppermute x4, starting transfers between devices, gather_slots(): lax.ppermute(block, ('core', 'xl', 'yh'), from_ahead(j))  19.5 us
    ppermute x3, starting transfers between devices, gather_half(): lax.ppermute(block, 'zh', step)  18.5 us
    ppermute x3, waiting for transfers between devices, gather_half(): lax.ppermute(block, 'zh', step)  13.3 us
    ppermute x3, waiting for transfers between devices, gather_half(): lax.ppermute(block, ('zl', 'yl'), flip)  11.8 us
    ppermute x3, starting transfers between devices, finish_terms(): lax.ppermute(own, 'xh', [(k, k ^ bits) for k in range(4)])  11.7 us
    pallas_call x1, Pallas kernels, layer_of(): pl.pallas_call(layer_kernel, out_shape=(jax.ShapeDtypeStruct(latents.shap...  10.2 us
    all_to_all x1, starting transfers between devices, body(): parts = lax.all_to_all(own, ('zh', 'yh'), 0, 0, tiled=True)  8.52 us
    ppermute x3, starting transfers between devices, gather_half(): lax.ppermute(block, ('zl', 'yl'), flip)  8.37 us
  transfers between devices with their start and end apart: 19, of which 8 were waited for; matrix products, arithmetic and copies ran while one was open for 0% of the time, Pallas kernels for 6%

profile of v4, /device:TPU:1, one launch (start us, length us, event | category | flops | bytes accessed | tf_op | source)
XLA Modules:
  0.0 159.7 jit_solution(3906916196449387865)
XLA Ops:
  5.1 7.7 %shard_map.85 = (f32[4,4,112,384]{3,2,1,0:T(8,128)S(1)}, bf16[4,4,112,384]{3,2,1,0:T(8,128)(2,1)S(1)}) custom-call(s32[4]{0:T(128)S(1)} %pad_add_fusion.here, bf16[480,384]{1,0:T(8,128)(2,1)S(1)} %bitcast.36, f32[1,384]{1,0:T(1,128)S(1)} %broadcast_in_dim.6.gain, f32[1,384]{1,0:T(1,128)S(1)} %broadcast_in_dim.7.bias, bf16[480,384]{1,0:T(8,128)(2,1)S(1)} %bitcast.38, ...), custom_call_target="tpu_custom_call" | custom-call | flops 4000000000 | bytes 8000000 | tf_op jit(solution)/shard_map/pallas_call | solution.py:223
  13.9 4.5 %collective-permute-start.1 = (bf16[28,384]{1,0:T(8,128)(2,1)S(1)}, bf16[28,384]{1,0:T(8,128)(2,1)S(1)}, u32[]{:S(2)}, u32[]{:S(2)}) collective-permute-start(bf16[28,384]{1,0:T(8,128)(2,1)S(1)} %pad.4), channel_id=1, source_target_pairs={{0,0},{128,8},{2,2},{130,10},{4,4},{132,12},{6,6},{134,14},{8,128}... | collective-permute-start | bytes 64520 | tf_op jit(solution)/shard_map/ppermute | solution.py:179
  18.4 6.3 %collective-permute-start.2 = (bf16[28,384]{1,0:T(8,128)(2,1)S(1)}, bf16[28,384]{1,0:T(8,128)(2,1)S(1)}, u32[]{:S(2)}, u32[]{:S(2)}) collective-permute-start(bf16[28,384]{1,0:T(8,128)(2,1)S(1)} %pad.4), channel_id=1, source_target_pairs={{2,0},{130,8},{4,2},{132,10},{6,4},{134,12},{0,6},{128,14},{10,128... | collective-permute-start | bytes 64520 | tf_op jit(solution)/shard_map/ppermute | solution.py:179
  24.7 4.5 %collective-permute-start.3 = (bf16[28,384]{1,0:T(8,128)(2,1)S(1)}, bf16[28,384]{1,0:T(8,128)(2,1)S(1)}, u32[]{:S(2)}, u32[]{:S(2)}) collective-permute-start(bf16[28,384]{1,0:T(8,128)(2,1)S(1)} %pad.4), channel_id=1, source_target_pairs={{4,0},{132,8},{6,2},{134,10},{0,4},{128,12},{2,6},{130,14},{12,128... | collective-permute-start | bytes 64520 | tf_op jit(solution)/shard_map/ppermute | solution.py:179
  29.3 4.2 %collective-permute-start.4 = (bf16[28,384]{1,0:T(8,128)(2,1)S(1)}, bf16[28,384]{1,0:T(8,128)(2,1)S(1)}, u32[]{:S(2)}, u32[]{:S(2)}) collective-permute-start(bf16[28,384]{1,0:T(8,128)(2,1)S(1)} %pad.4), channel_id=1, source_target_pairs={{6,0},{134,8},{0,2},{128,10},{2,4},{130,12},{4,6},{132,14},{14,128... | collective-permute-start | bytes 64520 | tf_op jit(solution)/shard_map/ppermute | solution.py:179
  33.5 5.9 %collective-permute-start = (bf16[4,4,112,384]{3,2,1,0:T(8,128)(2,1)}, bf16[4,4,112,384]{3,2,1,0:T(8,128)(2,1)}, u32[]{:S(2)}, u32[]{:S(2)}) collective-permute-start(bf16[4,4,112,384]{3,2,1,0:T(8,128)(2,1)} %copy-done), channel_id=1, source_target_pairs={{0,128},{128,0},{1,129},{129,1},{2,130},{130,2},{3,131},{131,3},{4... | collective-permute-start | bytes 4128776 | tf_op jit(solution)/shard_map/ppermute | solution.py:202
  39.6 2.9 %collective-permute-done = bf16[4,4,112,384]{3,2,1,0:T(8,128)(2,1)} collective-permute-done((bf16[4,4,112,384]{3,2,1,0:T(8,128)(2,1)}, bf16[4,4,112,384]{3,2,1,0:T(8,128)(2,1)}, u32[]{:S(2)}, u32[]{:S(2)}) %collective-permute-start) | collective-permute-done | bytes 1376288 | tf_op jit(solution)/shard_map/ppermute | solution.py:202
  42.4 2.8 %add_convert_fusion = bf16[4,4,112,384]{3,2,1,0:T(8,128)(2,1)} fusion(f32[4,4,112,384]{3,2,1,0:T(8,128)S(1)} %get-tuple-element.19, bf16[4,4,112,384]{3,2,1,0:T(8,128)(2,1)} %collective-permute-done), kind=kLoop, calls=%fused_computation | loop fusion | flops 2064384 | bytes 5505024 | tf_op jit(solution)/shard_map/convert_element_type | solution.py:203
  45.3 3.5 %all-to-all-start = ((bf16[4,4,112,384]{3,2,1,0:T(8,128)(2,1)}), bf16[4,4,112,384]{3,2,1,0:T(8,128)(2,1)S(1)}, u32[]{:S(2)}, u32[]{:S(2)}) async-start(bf16[4,4,112,384]{3,2,1,0:T(8,128)(2,1)} %add_convert_fusion), calls=%async_computation | async-start | bytes 2752512 | tf_op jit(solution)/shard_map/all_to_all | solution.py:207
  48.8 5.0 %collective-permute-start.7 = (bf16[112,384]{1,0:T(8,128)(2,1)S(1)}, bf16[112,384]{1,0:T(8,128)(2,1)S(1)}, u32[]{:S(2)}, u32[]{:S(2)}) collective-permute-start(bf16[112,384]{1,0:T(8,128)(2,1)S(1)} %reshape.32), channel_id=1, source_target_pairs={{96,0},{0,32},{32,64},{64,96},{97,1},{1,33},{33,65},{65,97},{98,2}... | collective-permute-start | bytes 258056 | tf_op jit(solution)/shard_map/ppermute | solution.py:187
  53.8 11.6 %collective-permute-start.6 = (bf16[112,384]{1,0:T(8,128)(2,1)S(1)}, bf16[112,384]{1,0:T(8,128)(2,1)S(1)}, u32[]{:S(2)}, u32[]{:S(2)}) collective-permute-start(bf16[112,384]{1,0:T(8,128)(2,1)S(1)} %reshape.32), channel_id=1, source_target_pairs={{64,0},{96,32},{0,64},{32,96},{65,1},{97,33},{1,65},{33,97},{66,2}... | collective-permute-start | bytes 258056 | tf_op jit(solution)/shard_map/ppermute | solution.py:187
  67.3 11.5 %collective-permute-done.7 = bf16[112,384]{1,0:T(8,128)(2,1)S(1)} collective-permute-done((bf16[112,384]{1,0:T(8,128)(2,1)S(1)}, bf16[112,384]{1,0:T(8,128)(2,1)S(1)}, u32[]{:S(2)}, u32[]{:S(2)}) %collective-permute-start.7) | collective-permute-done | bytes 86048 | tf_op jit(solution)/shard_map/ppermute | solution.py:187
  82.7 4.2 %collective-permute-start.9 = (bf16[4,112,384]{2,1,0:T(8,128)(2,1)S(1)}, bf16[4,112,384]{2,1,0:T(8,128)(2,1)S(1)}, u32[]{:S(2)}, u32[]{:S(2)}) collective-permute-start(bf16[4,112,384]{2,1,0:T(8,128)(2,1)S(1)} %get-tuple-element.35), channel_id=1, source_target_pairs={{16,0},{17,1},{0,16},{1,17},{18,2},{19,3},{2,18},{3,19},{20,4},{21... | collective-permute-start | bytes 1032200 | tf_op jit(solution)/shard_map/ppermute | solution.py:189
  86.9 2.2 %collective-permute-start.8 = (bf16[4,112,384]{2,1,0:T(8,128)(2,1)S(1)}, bf16[4,112,384]{2,1,0:T(8,128)(2,1)S(1)}, u32[]{:S(2)}, u32[]{:S(2)}) collective-permute-start(bf16[4,112,384]{2,1,0:T(8,128)(2,1)S(1)} %get-tuple-element.35), channel_id=1, source_target_pairs={{1,0},{0,1},{17,16},{16,17},{3,2},{2,3},{19,18},{18,19},{5,4},{4,5... | collective-permute-start | bytes 1032200 | tf_op jit(solution)/shard_map/ppermute | solution.py:189
  89.1 2.5 %collective-permute-done.10 = bf16[4,112,384]{2,1,0:T(8,128)(2,1)S(1)} collective-permute-done((bf16[4,112,384]{2,1,0:T(8,128)(2,1)S(1)}, bf16[4,112,384]{2,1,0:T(8,128)(2,1)S(1)}, u32[]{:S(2)}, u32[]{:S(2)}) %collective-permute-start.10) | collective-permute-done | bytes 344096 | tf_op jit(solution)/shard_map/ppermute | solution.py:189
  91.6 9.3 %collective-permute-done.9 = bf16[4,112,384]{2,1,0:T(8,128)(2,1)S(1)} collective-permute-done((bf16[4,112,384]{2,1,0:T(8,128)(2,1)S(1)}, bf16[4,112,384]{2,1,0:T(8,128)(2,1)S(1)}, u32[]{:S(2)}, u32[]{:S(2)}) %collective-permute-start.9) | collective-permute-done | bytes 344096 | tf_op jit(solution)/shard_map/ppermute | solution.py:189
  103.9 2.4 %collective-permute-start.11 = (bf16[4,4,112,384]{3,2,1,0:T(8,128)(2,1)S(1)}, bf16[4,4,112,384]{3,2,1,0:T(8,128)(2,1)S(1)}, u32[]{:S(2)}, u32[]{:S(2)}) collective-permute-start(bf16[4,4,112,384]{3,2,1,0:T(8,128)(2,1)S(1)} %pad_maximum_fusion.held), channel_id=1, source_target_pairs={{0,128},{128,0},{1,129},{129,1},{2,130},{130,2},{3,131},{131,3},{4... | collective-permute-start | bytes 4128776 | tf_op jit(solution)/shard_map/ppermute | solution.py:279
  106.3 8.5 %all-to-all-start.1 = ((bf16[16,28,384]{2,1,0:T(8,128)(2,1)}), bf16[16,28,384]{2,1,0:T(8,128)(2,1)}, u32[]{:S(2)}, u32[]{:S(2)}) async-start(bf16[16,28,384]{2,1,0:T(8,128)(2,1)} %convert_element_type.18), calls=%async_computation.1 | async-start | bytes 786432 | tf_op jit(solution)/shard_map/all_to_all | solution.py:278
  115.9 10.2 %shard_map.86 = (bf16[480,384]{1,0:T(8,128)(2,1)}, bf16[480,384]{1,0:T(8,128)(2,1)}) custom-call(s32[4]{0:T(128)S(1)} %pad_add_fusion.here, bf16[480,384]{1,0:T(8,128)(2,1)S(1)} %bitcast.37, f32[1,384]{1,0:T(1,128)S(1)} %broadcast_in_dim.6.gain, f32[1,384]{1,0:T(1,128)S(1)} %broadcast_in_dim.7.bias, bf16[480,384]{1,0:T(8,128)(2,1)S(1)} %bitcast.39, ...), custom_call_target="tpu_custom_call" | custom-call | flops 4000000000 | bytes 8000000 | tf_op jit(solution)/shard_map/pallas_call | solution.py:246
  126.0 3.6 %all-to-all-done.1 = bf16[16,28,384]{2,1,0:T(8,128)(2,1)} async-done(((bf16[16,28,384]{2,1,0:T(8,128)(2,1)}), bf16[16,28,384]{2,1,0:T(8,128)(2,1)}, u32[]{:S(2)}, u32[]{:S(2)}) %all-to-all-start.1) | async-done | bytes 344096 | tf_op jit(solution)/shard_map/all_to_all | solution.py:278
  130.7 4.0 %collective-permute-start.13 = (f32[28,384]{1,0:T(8,128)S(1)}, f32[28,384]{1,0:T(8,128)S(1)}, u32[]{:S(2)}, u32[]{:S(2)}) collective-permute-start(f32[28,384]{1,0:T(8,128)S(1)} %convert_reduce_fusion), channel_id=1, source_target_pairs={{0,256},{256,0},{512,768},{768,512},{1,257},{257,1},{513,769},{769... | collective-permute-start | bytes 129032 | tf_op jit(solution)/shard_map/ppermute | solution.py:214
  134.8 5.6 %collective-permute-start.14 = (f32[28,384]{1,0:T(8,128)S(1)}, f32[28,384]{1,0:T(8,128)S(1)}, u32[]{:S(2)}, u32[]{:S(2)}) collective-permute-start(f32[28,384]{1,0:T(8,128)S(1)} %convert_reduce_fusion), channel_id=1, source_target_pairs={{0,768},{256,512},{512,256},{768,0},{1,769},{257,513},{513,257},{7... | collective-permute-start | bytes 129032 | tf_op jit(solution)/shard_map/ppermute | solution.py:214
  142.5 7.1 %collective-permute-done.12 = f32[28,384]{1,0:T(8,128)S(1)} collective-permute-done((f32[28,384]{1,0:T(8,128)S(1)}, f32[28,384]{1,0:T(8,128)S(1)}, u32[]{:S(2)}, u32[]{:S(2)}) %collective-permute-start.12) | collective-permute-done | bytes 43040 | tf_op jit(solution)/shard_map/ppermute | solution.py:214
  149.6 6.3 %collective-permute-start.16 = (f32[28,384]{1,0:T(8,128)S(1)}, f32[28,384]{1,0:T(8,128)S(1)}, u32[]{:S(2)}, u32[]{:S(2)}) collective-permute-start(f32[28,384]{1,0:T(8,128)S(1)} %add_add_fusion), channel_id=1, source_target_pairs={{0,0},{8,128},{128,8},{136,136},{1,1},{9,129},{129,9},{137,137},{2... | collective-permute-start | bytes 129032 | tf_op jit(solution)/shard_map/ppermute | solution.py:218
  (57 shorter events, 22.3 us)
Async XLA Ops:
  5.1 8.8 %copy-start.7 = (bf16[3,9,384]{2,0,1:T(4,128)(2,1)S(1)}, bf16[3,9,384]{2,0,1:T(4,128)(2,1)}, u32[]{:S(2)}) copy-start(bf16[3,9,384]{2,0,1:T(4,128)(2,1)} %param.9) | copy-start | bytes 62212
  12.8 1.1 copy-start
  13.9 25.4 %collective-permute-start.1 = (bf16[28,384]{1,0:T(8,128)(2,1)S(1)}, bf16[28,384]{1,0:T(8,128)(2,1)S(1)}, u32[]{:S(2)}, u32[]{:S(2)}) collective-permute-start(bf16[28,384]{1,0:T(8,128)(2,1)S(1)} %pad.4), channel_id=1, source_target_pairs={{0,0},{128,8},{2,2},{130,10},{4,4},{132,12},{6,6},{134,14},{8,128}... | collective-permute-start | bytes 64520 | tf_op jit(solution)/shard_map/ppermute | solution.py:179
  18.4 20.9 %collective-permute-start.2 = (bf16[28,384]{1,0:T(8,128)(2,1)S(1)}, bf16[28,384]{1,0:T(8,128)(2,1)S(1)}, u32[]{:S(2)}, u32[]{:S(2)}) collective-permute-start(bf16[28,384]{1,0:T(8,128)(2,1)S(1)} %pad.4), channel_id=1, source_target_pairs={{2,0},{130,8},{4,2},{132,10},{6,4},{134,12},{0,6},{128,14},{10,128... | collective-permute-start | bytes 64520 | tf_op jit(solution)/shard_map/ppermute | solution.py:179
  24.7 14.7 %collective-permute-start.3 = (bf16[28,384]{1,0:T(8,128)(2,1)S(1)}, bf16[28,384]{1,0:T(8,128)(2,1)S(1)}, u32[]{:S(2)}, u32[]{:S(2)}) collective-permute-start(bf16[28,384]{1,0:T(8,128)(2,1)S(1)} %pad.4), channel_id=1, source_target_pairs={{4,0},{132,8},{6,2},{134,10},{0,4},{128,12},{2,6},{130,14},{12,128... | collective-permute-start | bytes 64520 | tf_op jit(solution)/shard_map/ppermute | solution.py:179
  29.3 10.2 %collective-permute-start.4 = (bf16[28,384]{1,0:T(8,128)(2,1)S(1)}, bf16[28,384]{1,0:T(8,128)(2,1)S(1)}, u32[]{:S(2)}, u32[]{:S(2)}) collective-permute-start(bf16[28,384]{1,0:T(8,128)(2,1)S(1)} %pad.4), channel_id=1, source_target_pairs={{6,0},{134,8},{0,2},{128,10},{2,4},{130,12},{4,6},{132,14},{14,128... | collective-permute-start | bytes 64520 | tf_op jit(solution)/shard_map/ppermute | solution.py:179
  33.5 9.0 %collective-permute-start = (bf16[4,4,112,384]{3,2,1,0:T(8,128)(2,1)}, bf16[4,4,112,384]{3,2,1,0:T(8,128)(2,1)}, u32[]{:S(2)}, u32[]{:S(2)}) collective-permute-start(bf16[4,4,112,384]{3,2,1,0:T(8,128)(2,1)} %copy-done), channel_id=1, source_target_pairs={{0,128},{128,0},{1,129},{129,1},{2,130},{130,2},{3,131},{131,3},{4... | collective-permute-start | bytes 4128776 | tf_op jit(solution)/shard_map/ppermute | solution.py:202
  45.3 55.9 %all-to-all-start = ((bf16[4,4,112,384]{3,2,1,0:T(8,128)(2,1)}), bf16[4,4,112,384]{3,2,1,0:T(8,128)(2,1)S(1)}, u32[]{:S(2)}, u32[]{:S(2)}) async-start(bf16[4,4,112,384]{3,2,1,0:T(8,128)(2,1)} %add_convert_fusion), calls=%async_computation | async-start | bytes 2752512 | tf_op jit(solution)/shard_map/all_to_all | solution.py:207
  48.8 30.0 %collective-permute-start.7 = (bf16[112,384]{1,0:T(8,128)(2,1)S(1)}, bf16[112,384]{1,0:T(8,128)(2,1)S(1)}, u32[]{:S(2)}, u32[]{:S(2)}) collective-permute-start(bf16[112,384]{1,0:T(8,128)(2,1)S(1)} %reshape.32), channel_id=1, source_target_pairs={{96,0},{0,32},{32,64},{64,96},{97,1},{1,33},{33,65},{65,97},{98,2}... | collective-permute-start | bytes 258056 | tf_op jit(solution)/shard_map/ppermute | solution.py:187
  53.8 26.9 %collective-permute-start.6 = (bf16[112,384]{1,0:T(8,128)(2,1)S(1)}, bf16[112,384]{1,0:T(8,128)(2,1)S(1)}, u32[]{:S(2)}, u32[]{:S(2)}) collective-permute-start(bf16[112,384]{1,0:T(8,128)(2,1)S(1)} %reshape.32), channel_id=1, source_target_pairs={{64,0},{96,32},{0,64},{32,96},{65,1},{97,33},{1,65},{33,97},{66,2}... | collective-permute-start | bytes 258056 | tf_op jit(solution)/shard_map/ppermute | solution.py:187
  65.4 15.3 %collective-permute-start.5 = (bf16[112,384]{1,0:T(8,128)(2,1)S(1)}, bf16[112,384]{1,0:T(8,128)(2,1)S(1)}, u32[]{:S(2)}, u32[]{:S(2)}) collective-permute-start(bf16[112,384]{1,0:T(8,128)(2,1)S(1)} %reshape.32), channel_id=1, source_target_pairs={{32,0},{64,32},{96,64},{0,96},{33,1},{65,33},{97,65},{1,97},{34,2}... | collective-permute-start | bytes 258056 | tf_op jit(solution)/shard_map/ppermute | solution.py:187
  80.7 10.9 %collective-permute-start.10 = (bf16[4,112,384]{2,1,0:T(8,128)(2,1)S(1)}, bf16[4,112,384]{2,1,0:T(8,128)(2,1)S(1)}, u32[]{:S(2)}, u32[]{:S(2)}) collective-permute-start(bf16[4,112,384]{2,1,0:T(8,128)(2,1)S(1)} %get-tuple-element.35), channel_id=1, source_target_pairs={{17,0},{16,1},{1,16},{0,17},{19,2},{18,3},{3,18},{2,19},{21,4},{20... | collective-permute-start | bytes 1032200 | tf_op jit(solution)/shard_map/ppermute | solution.py:189
  82.7 18.2 %collective-permute-start.9 = (bf16[4,112,384]{2,1,0:T(8,128)(2,1)S(1)}, bf16[4,112,384]{2,1,0:T(8,128)(2,1)S(1)}, u32[]{:S(2)}, u32[]{:S(2)}) collective-permute-start(bf16[4,112,384]{2,1,0:T(8,128)(2,1)S(1)} %get-tuple-element.35), channel_id=1, source_target_pairs={{16,0},{17,1},{0,16},{1,17},{18,2},{19,3},{2,18},{3,19},{20,4},{21... | collective-permute-start | bytes 1032200 | tf_op jit(solution)/shard_map/ppermute | solution.py:189
  86.9 14.0 %collective-permute-start.8 = (bf16[4,112,384]{2,1,0:T(8,128)(2,1)S(1)}, bf16[4,112,384]{2,1,0:T(8,128)(2,1)S(1)}, u32[]{:S(2)}, u32[]{:S(2)}) collective-permute-start(bf16[4,112,384]{2,1,0:T(8,128)(2,1)S(1)} %get-tuple-element.35), channel_id=1, source_target_pairs={{1,0},{0,1},{17,16},{16,17},{3,2},{2,3},{19,18},{18,19},{5,4},{4,5... | collective-permute-start | bytes 1032200 | tf_op jit(solution)/shard_map/ppermute | solution.py:189
  101.1 13.8 %copy-start.2 = (bf16[1,24,20,384]{3,1,2,0:T(8,128)(2,1)S(1)}, bf16[1,24,20,384]{3,1,2,0:T(8,128)(2,1)}, u32[]{:S(2)}) copy-start(bf16[1,24,20,384]{3,1,2,0:T(8,128)(2,1)} %param.6) | copy-start | bytes 1105924
  101.1 13.8 %copy-start.4 = (bf16[1,24,20,384]{3,1,2,0:T(8,128)(2,1)S(1)}, bf16[1,24,20,384]{3,1,2,0:T(8,128)(2,1)}, u32[]{:S(2)}) copy-start(bf16[1,24,20,384]{3,1,2,0:T(8,128)(2,1)} %param.10) | copy-start | bytes 1105924
  103.9 10.9 %collective-permute-start.11 = (bf16[4,4,112,384]{3,2,1,0:T(8,128)(2,1)S(1)}, bf16[4,4,112,384]{3,2,1,0:T(8,128)(2,1)S(1)}, u32[]{:S(2)}, u32[]{:S(2)}) collective-permute-start(bf16[4,4,112,384]{3,2,1,0:T(8,128)(2,1)S(1)} %pad_maximum_fusion.held), channel_id=1, source_target_pairs={{0,128},{128,0},{1,129},{129,1},{2,130},{130,2},{3,131},{131,3},{4... | collective-permute-start | bytes 4128776 | tf_op jit(solution)/shard_map/ppermute | solution.py:279
  106.3 23.4 %all-to-all-start.1 = ((bf16[16,28,384]{2,1,0:T(8,128)(2,1)}), bf16[16,28,384]{2,1,0:T(8,128)(2,1)}, u32[]{:S(2)}, u32[]{:S(2)}) async-start(bf16[16,28,384]{2,1,0:T(8,128)(2,1)} %convert_element_type.18), calls=%async_computation.1 | async-start | bytes 786432 | tf_op jit(solution)/shard_map/all_to_all | solution.py:278
  114.9 1.0 copy-start.6
  130.7 11.7 %collective-permute-start.13 = (f32[28,384]{1,0:T(8,128)S(1)}, f32[28,384]{1,0:T(8,128)S(1)}, u32[]{:S(2)}, u32[]{:S(2)}) collective-permute-start(f32[28,384]{1,0:T(8,128)S(1)} %convert_reduce_fusion), channel_id=1, source_target_pairs={{0,256},{256,0},{512,768},{768,512},{1,257},{257,1},{513,769},{769... | collective-permute-start | bytes 129032 | tf_op jit(solution)/shard_map/ppermute | solution.py:214
  134.8 7.7 %collective-permute-start.14 = (f32[28,384]{1,0:T(8,128)S(1)}, f32[28,384]{1,0:T(8,128)S(1)}, u32[]{:S(2)}, u32[]{:S(2)}) collective-permute-start(f32[28,384]{1,0:T(8,128)S(1)} %convert_reduce_fusion), channel_id=1, source_target_pairs={{0,768},{256,512},{512,256},{768,0},{1,769},{257,513},{513,257},{7... | collective-permute-start | bytes 129032 | tf_op jit(solution)/shard_map/ppermute | solution.py:214
  140.4 9.1 %collective-permute-start.12 = (f32[28,384]{1,0:T(8,128)S(1)}, f32[28,384]{1,0:T(8,128)S(1)}, u32[]{:S(2)}, u32[]{:S(2)}) collective-permute-start(f32[28,384]{1,0:T(8,128)S(1)} %convert_reduce_fusion), channel_id=1, source_target_pairs={{0,512},{256,768},{512,0},{768,256},{1,513},{257,769},{513,1},{769... | collective-permute-start | bytes 129032 | tf_op jit(solution)/shard_map/ppermute | solution.py:214
  149.6 8.2 %collective-permute-start.16 = (f32[28,384]{1,0:T(8,128)S(1)}, f32[28,384]{1,0:T(8,128)S(1)}, u32[]{:S(2)}, u32[]{:S(2)}) collective-permute-start(f32[28,384]{1,0:T(8,128)S(1)} %add_add_fusion), channel_id=1, source_target_pairs={{0,0},{8,128},{128,8},{136,136},{1,1},{9,129},{129,9},{137,137},{2... | collective-permute-start | bytes 129032 | tf_op jit(solution)/shard_map/ppermute | solution.py:218
  155.9 3.1 %collective-permute-start.15 = (f32[28,384]{1,0:T(8,128)S(1)}, f32[28,384]{1,0:T(8,128)S(1)}, u32[]{:S(2)}, u32[]{:S(2)}) collective-permute-start(f32[28,384]{1,0:T(8,128)S(1)} %add_add_fusion), channel_id=1, source_target_pairs={{8,0},{128,136},{136,8},{0,128},{9,1},{129,137},{137,9},{1,129},{1... | collective-permute-start | bytes 129032 | tf_op jit(solution)/shard_map/ppermute | solution.py:218
  (3 other events, 3.0 us)

commit v5 on v3

--- a/solution.py
+++ b/solution.py
@@ -177,13 +177,11 @@
     return lax.all_to_all(copies, axis, 0, 0, tiled=True)
 
 
-def gather_halves(conv_weight):
+def gather_slots(conv_weight):
     taps, rows, chans = conv_weight.shape
     block = jnp.pad(conv_weight.reshape(taps * rows, chans), ((0, SLOT - taps * rows), (0, 0)))
     block = lax.ppermute(block, ("core", "xl"), SWAP)
-    block = spread(block, ("zh", "yh")).reshape(PACKED[1:])
-    held = spread(block, ("zl", "yl"))
-    return held, lax.ppermute(held, "core", TRADE)
+    return lax.all_gather(block, ("zh", "yh")).reshape(PACKED[1:])
 
 
 def halve_terms(keep, send):
@@ -254,13 +252,15 @@
     core = lax.axis_index("core").reshape(1)
     gain, bias = norm_gain[None], norm_bias[None]
     sel = jnp.asarray(SEL, jnp.bfloat16)
-    held, got = gather_halves(conv_weight)
+    block = gather_slots(conv_weight)
     latents, cotangent = columns_first(latents), columns_first(cotangent)
     keep, send = terms_of(core, latents, gain, bias, cotangent, sel)
     parts = halve_terms(keep, send)
+    parts, block = lax.optimization_barrier((parts, block))
+    held = spread(block, ("zl", "yl"))
+    got = lax.ppermute(held, "core", TRADE)
+    grad_weight = finish_terms(parts) * scale
     output, grad_input = layer_of(core, latents, gain, bias, cotangent, held, got, sel)
-    parts, output, grad_input = lax.optimization_barrier((parts, output, grad_input))
-    grad_weight = finish_terms(parts) * scale
     return (rows_first(output), rows_first(grad_input), grad_weight)
 
 

time: 139 us -> 175 us (1.26); the launches traced: 137 us -> 175 us
  blocking collectives: 0 us -> 79.8 us
  waiting for transfers between devices: 45 us -> 9.42 us
  starting transfers between devices: 63 us -> 57.8 us
  other arithmetic: 4.84 us -> 0.81 us
  local copies, waits for them, and re-layouts: 6.33 us -> 9.32 us
    all_gather x0 -> x1, blocking collectives: none -> 44 us  [gather_slots(): return lax.all_gather(block, ('zh', 'yh')).reshape(PACKED[1:])]
    all_to_all x0 -> x2, blocking collectives: none -> 35.8 us  [the longest x1 19.8 us: halve_terms(): lax.all_to_all(own, ('zl', 'yl'), 0, 0, tiled=True).astype(jnp.float32)]
    all_to_all x3 -> x0, waiting for transfers between devices: 32.4 us -> none  [the longest x2 16.8 us: spread(): return lax.all_to_all(copies, axis, 0, 0, tiled=True)]
    all_to_all x3 -> x0, starting transfers between devices: 29.3 us -> none  [the longest x2 25 us: spread(): return lax.all_to_all(copies, axis, 0, 0, tiled=True)]
    ppermute x1, starting transfers between devices: 1.92 us -> 16.1 us  [halve_terms(): got = lax.ppermute(send, 'core', TRADE)]
    ppermute x2, starting transfers between devices: 6.43 us -> 12.5 us  [the longest x1 7.3 us: body(): got = lax.ppermute(held, 'core', TRADE)]
    all_to_all x1, starting transfers between devices: 5.07 us -> 9.1 us  [halve_terms(): return lax.all_to_all(own, ('zh', 'yh'), 0, 0, tiled=True)]
    unnamed x14 -> x20, local copies, waits for them, and re-layouts: 2.44 us -> 6.3 us
  transfers between devices with their start and end apart: 11 -> 8, of which waited for: 9 -> 5; matrix products, arithmetic and copies ran while one was open for 4% -> 1% of each run, Pallas kernels for 12% -> 0%
where the time goes in v5:
time: 175 us
  blocking collectives  79.8 us (46%)
  starting transfers between devices  57.8 us (33%)
  Pallas kernels  16.5 us (9%)
  waiting for transfers between devices  9.42 us (5%)
  local copies, waits for them, and re-layouts  9.32 us (5%)
    all_gather x1, blocking collectives, gather_slots(): return lax.all_gather(block, ('zh', 'yh')).reshape(PACKED[1:])  44 us
    all_to_all x1, blocking collectives, halve_terms(): lax.all_to_all(own, ('zl', 'yl'), 0, 0, tiled=True).astype(jnp.float32)  19.8 us
    ppermute x1, starting transfers between devices, halve_terms(): got = lax.ppermute(send, 'core', TRADE)  16.1 us
    all_to_all x1, blocking collectives, spread(): return lax.all_to_all(copies, axis, 0, 0, tiled=True)  15.9 us
    ppermute x2, starting transfers between devices, finish_terms(): own = own + lax.ppermute(own, 'xh', [(k, k ^ bit) for k in range(4)])  11 us
    pallas_call x1, Pallas kernels, layer_of(): pl.pallas_call(layer_kernel, out_shape=(jax.ShapeDtypeStruct(latents.shap...  9.64 us
    ppermute x2, starting transfers between devices, finish_terms(): own = lax.ppermute(own, pair, NEAR) + lax.ppermute(own, pair, SWAP)  9.15 us
    all_to_all x1, starting transfers between devices, halve_terms(): return lax.all_to_all(own, ('zh', 'yh'), 0, 0, tiled=True)  9.1 us
  transfers between devices with their start and end apart: 8, of which 5 were waited for; matrix products, arithmetic and copies ran while one was open for 1% of the time, Pallas kernels for 0%

profile of v5, /device:TPU:1, one launch (start us, length us, event | category | flops | bytes accessed | tf_op | source)
XLA Modules:
  0.0 174.5 jit_solution(13103838177494539362)
XLA Ops:
  2.0 1.0 copy-done
  3.0 1.0 copy-done.2
  4.0 1.0 copy-done.4
  5.0 6.9 %shard_map.85 = (f32[4,4,112,384]{3,2,1,0:T(8,128)S(1)}, bf16[4,4,112,384]{3,2,1,0:T(8,128)(2,1)S(1)}) custom-call(s32[1]{0:T(128)} %bitcast.core, bf16[480,384]{1,0:T(8,128)(2,1)S(1)} %bitcast.14, f32[1,384]{1,0:T(1,128)S(1)} %broadcast_in_dim.12.gain, f32[1,384]{1,0:T(1,128)S(1)} %broadcast_in_dim.13.bias, bf16[480,384]{1,0:T(8,128)(2,1)S(1)} %bitcast.16, ...), custom_call_target="tpu_custom_call" | custom-call | flops 4000000000 | bytes 8000000 | tf_op jit(solution)/shard_map/pallas_call | solution.py:205
  11.9 16.1 %collective-permute-start = (bf16[4,4,112,384]{3,2,1,0:T(8,128)(2,1)S(1)}, bf16[4,4,112,384]{3,2,1,0:T(8,128)(2,1)S(1)}, u32[]{:S(2)}, u32[]{:S(2)}) collective-permute-start(bf16[4,4,112,384]{3,2,1,0:T(8,128)(2,1)S(1)} %get-tuple-element.10), channel_id=1, source_target_pairs={{0,128},{128,0},{1,129},{129,1},{2,130},{130,2},{3,131},{131,3},{4... | collective-permute-start | bytes 4128776 | tf_op jit(solution)/shard_map/ppermute | solution.py:188
  28.0 2.7 %collective-permute-done = bf16[4,4,112,384]{3,2,1,0:T(8,128)(2,1)S(1)} collective-permute-done((bf16[4,4,112,384]{3,2,1,0:T(8,128)(2,1)S(1)}, bf16[4,4,112,384]{3,2,1,0:T(8,128)(2,1)S(1)}, u32[]{:S(2)}, u32[]{:S(2)}) %collective-permute-start) | collective-permute-done | bytes 1376288 | tf_op jit(solution)/shard_map/ppermute | solution.py:188
  31.1 19.8 %all_to_all.15 = bf16[4,4,112,384]{3,2,1,0:T(8,128)(2,1)S(1)} all-to-all(bf16[4,4,112,384]{3,2,1,0:T(8,128)(2,1)S(1)} %add_convert_fusion), channel_id=1, replica_groups=mesh['xh'=4,'core'=2,'zh'=4,'zl'=2,'xl'=2,'yh'=4,'yl'=2] {'zl','yl'}, dimensions={0} | all-to-all | bytes 2752512 | tf_op jit(solution)/shard_map/all_to_all | solution.py:190
  51.2 0.8 convert_element_type.18
  52.0 9.1 %all-to-all-start.1 = ((bf16[16,28,384]{2,1,0:T(8,128)(2,1)}), bf16[16,28,384]{2,1,0:T(8,128)(2,1)S(1)}, u32[]{:S(2)}, u32[]{:S(2)}) async-start(bf16[16,28,384]{2,1,0:T(8,128)(2,1)} %convert_element_type.18), calls=%async_computation.1 | async-start | bytes 786432 | tf_op jit(solution)/shard_map/all_to_all | solution.py:192
  61.2 5.2 %collective-permute-start.1 = (bf16[28,384]{1,0:T(8,128)(2,1)S(1)}, bf16[28,384]{1,0:T(8,128)(2,1)S(1)}, u32[]{:S(2)}, u32[]{:S(2)}) collective-permute-start(bf16[28,384]{1,0:T(8,128)(2,1)S(1)} %pad.4), channel_id=1, source_target_pairs={{0,0},{8,128},{128,8},{136,136},{1,1},{9,129},{129,9},{137,137},{2... | collective-permute-start | bytes 64520 | tf_op jit(solution)/shard_map/ppermute | solution.py:183
  66.4 1.8 %collective-permute-done.1 = bf16[28,384]{1,0:T(8,128)(2,1)S(1)} collective-permute-done((bf16[28,384]{1,0:T(8,128)(2,1)S(1)}, bf16[28,384]{1,0:T(8,128)(2,1)S(1)}, u32[]{:S(2)}, u32[]{:S(2)}) %collective-permute-start.1) | collective-permute-done | bytes 21536 | tf_op jit(solution)/shard_map/ppermute | solution.py:183
  68.2 44.0 %all-gather.1 = bf16[16,28,384]{2,1,0:T(8,128)(2,1)S(1)} all-gather(bf16[1,28,384]{2,1,0:T(8,128)(2,1)S(1)} %bitcast.18), channel_id=2, replica_groups=mesh['xh'=4,'core'=2,'zh'=4,'zl'=2,'xl'=2,'yh'=4,'yl'=2] {'zh','yh'}, dimensions={0}, use_global_device_ids=true | all-gather | bytes 365568 | tf_op jit(solution)/shard_map/all_gather | solution.py:184
  113.2 15.9 %all_to_all.16.held = bf16[4,4,112,384]{3,2,1,0:T(8,128)(2,1)S(1)} all-to-all(bf16[4,4,112,384]{3,2,1,0:T(8,128)(2,1)S(1)} %broadcast_in_dim.14), channel_id=1, replica_groups=mesh['xh'=4,'core'=2,'zh'=4,'zl'=2,'xl'=2,'yh'=4,'yl'=2] {'zl','yl'}, dimensions={0} | all-to-all | bytes 2752512 | tf_op jit(solution)/shard_map/all_to_all | solution.py:177
  129.2 7.3 %collective-permute-start.2 = (bf16[4,4,112,384]{3,2,1,0:T(8,128)(2,1)S(1)}, bf16[4,4,112,384]{3,2,1,0:T(8,128)(2,1)S(1)}, u32[]{:S(2)}, u32[]{:S(2)}) collective-permute-start(bf16[4,4,112,384]{3,2,1,0:T(8,128)(2,1)S(1)} %all_to_all.16.held), channel_id=1, source_target_pairs={{0,128},{128,0},{1,129},{129,1},{2,130},{130,2},{3,131},{131,3},{4... | collective-permute-start | bytes 4128776 | tf_op jit(solution)/shard_map/ppermute | solution.py:261
  136.5 4.1 %collective-permute-start.3 = (f32[28,384]{1,0:T(8,128)S(1)}, f32[28,384]{1,0:T(8,128)S(1)}, u32[]{:S(2)}, u32[]{:S(2)}) collective-permute-start(f32[28,384]{1,0:T(8,128)S(1)} %convert_reduce_fusion), channel_id=1, source_target_pairs={{0,256},{256,0},{512,768},{768,512},{1,257},{257,1},{513,769},{769... | collective-permute-start | bytes 129032 | tf_op jit(solution)/shard_map/ppermute | solution.py:198
  140.7 2.0 %collective-permute-done.3 = f32[28,384]{1,0:T(8,128)S(1)} collective-permute-done((f32[28,384]{1,0:T(8,128)S(1)}, f32[28,384]{1,0:T(8,128)S(1)}, u32[]{:S(2)}, u32[]{:S(2)}) %collective-permute-start.3) | collective-permute-done | bytes 43040 | tf_op jit(solution)/shard_map/ppermute | solution.py:198
  142.7 6.9 %collective-permute-start.4 = (f32[28,384]{1,0:T(8,128)S(1)}, f32[28,384]{1,0:T(8,128)S(1)}, u32[]{:S(2)}, u32[]{:S(2)}) collective-permute-start(f32[28,384]{1,0:T(8,128)S(1)} %add.15), channel_id=1, source_target_pairs={{0,512},{256,768},{512,0},{768,256},{1,513},{257,769},{513,1},{769... | collective-permute-start | bytes 129032 | tf_op jit(solution)/shard_map/ppermute | solution.py:198
  149.6 1.9 %collective-permute-done.4 = f32[28,384]{1,0:T(8,128)S(1)} collective-permute-done((f32[28,384]{1,0:T(8,128)S(1)}, f32[28,384]{1,0:T(8,128)S(1)}, u32[]{:S(2)}, u32[]{:S(2)}) %collective-permute-start.4) | collective-permute-done | bytes 43040 | tf_op jit(solution)/shard_map/ppermute | solution.py:198
  151.5 7.0 %collective-permute-start.6 = (f32[28,384]{1,0:T(8,128)S(1)}, f32[28,384]{1,0:T(8,128)S(1)}, u32[]{:S(2)}, u32[]{:S(2)}) collective-permute-start(f32[28,384]{1,0:T(8,128)S(1)} %add.16), channel_id=1, source_target_pairs={{0,0},{8,128},{128,8},{136,136},{1,1},{9,129},{129,9},{137,137},{2... | collective-permute-start | bytes 129032 | tf_op jit(solution)/shard_map/ppermute | solution.py:200
  158.6 2.1 %collective-permute-start.5 = (f32[28,384]{1,0:T(8,128)S(1)}, f32[28,384]{1,0:T(8,128)S(1)}, u32[]{:S(2)}, u32[]{:S(2)}) collective-permute-start(f32[28,384]{1,0:T(8,128)S(1)} %add.16), channel_id=1, source_target_pairs={{8,0},{128,136},{136,8},{0,128},{9,1},{129,137},{137,9},{1,129},{1... | collective-permute-start | bytes 129032 | tf_op jit(solution)/shard_map/ppermute | solution.py:200
  160.7 1.0 collective-permute-done.5
  162.3 1.5 copy.12
  163.9 1.0 copy-done.5
  164.9 9.6 %shard_map.86 = (bf16[480,384]{1,0:T(8,128)(2,1)}, bf16[480,384]{1,0:T(8,128)(2,1)}) custom-call(s32[1]{0:T(128)} %bitcast.core, bf16[480,384]{1,0:T(8,128)(2,1)S(1)} %bitcast.15, f32[1,384]{1,0:T(1,128)S(1)} %broadcast_in_dim.12.gain, f32[1,384]{1,0:T(1,128)S(1)} %broadcast_in_dim.13.bias, bf16[480,384]{1,0:T(8,128)(2,1)S(1)} %bitcast.17, ...), custom_call_target="tpu_custom_call" | custom-call | flops 4000000000 | bytes 8000000 | tf_op jit(solution)/shard_map/pallas_call | solution.py:228
  (31 shorter events, 3.8 us)
Async XLA Ops:
  2.0 1.0 copy-start
  3.0 1.0 copy-start.2
  4.0 1.0 copy-start.4
  11.9 18.8 %collective-permute-start = (bf16[4,4,112,384]{3,2,1,0:T(8,128)(2,1)S(1)}, bf16[4,4,112,384]{3,2,1,0:T(8,128)(2,1)S(1)}, u32[]{:S(2)}, u32[]{:S(2)}) collective-permute-start(bf16[4,4,112,384]{3,2,1,0:T(8,128)(2,1)S(1)} %get-tuple-element.10), channel_id=1, source_target_pairs={{0,128},{128,0},{1,129},{129,1},{2,130},{130,2},{3,131},{131,3},{4... | collective-permute-start | bytes 4128776 | tf_op jit(solution)/shard_map/ppermute | solution.py:188
  50.9 10.3 %copy-start.8 = (bf16[3,9,384]{2,0,1:T(4,128)(2,1)S(1)}, bf16[3,9,384]{2,0,1:T(4,128)(2,1)}, u32[]{:S(2)}) copy-start(bf16[3,9,384]{2,0,1:T(4,128)(2,1)} %param.9) | copy-start | bytes 62212
  52.0 60.3 %all-to-all-start.1 = ((bf16[16,28,384]{2,1,0:T(8,128)(2,1)}), bf16[16,28,384]{2,1,0:T(8,128)(2,1)S(1)}, u32[]{:S(2)}, u32[]{:S(2)}) async-start(bf16[16,28,384]{2,1,0:T(8,128)(2,1)} %convert_element_type.18), calls=%async_computation.1 | async-start | bytes 786432 | tf_op jit(solution)/shard_map/all_to_all | solution.py:192
  61.2 7.0 %collective-permute-start.1 = (bf16[28,384]{1,0:T(8,128)(2,1)S(1)}, bf16[28,384]{1,0:T(8,128)(2,1)S(1)}, u32[]{:S(2)}, u32[]{:S(2)}) collective-permute-start(bf16[28,384]{1,0:T(8,128)(2,1)S(1)} %pad.4), channel_id=1, source_target_pairs={{0,0},{8,128},{128,8},{136,136},{1,1},{9,129},{129,9},{137,137},{2... | collective-permute-start | bytes 64520 | tf_op jit(solution)/shard_map/ppermute | solution.py:183
  112.3 0.7 copy-start.6
  113.2 23.3 %copy-start.7 = (bf16[16,28,384]{2,1,0:T(8,128)(2,1)S(1)}, bf16[16,28,384]{2,1,0:T(8,128)(2,1)}, u32[]{:S(2)}) copy-start(bf16[16,28,384]{2,1,0:T(8,128)(2,1)} %copy-done.6) | copy-start | bytes 1032196
  113.2 50.7 %copy-start.1 = (bf16[1,24,20,384]{3,1,2,0:T(8,128)(2,1)S(1)}, bf16[1,24,20,384]{3,1,2,0:T(8,128)(2,1)}, u32[]{:S(2)}) copy-start(bf16[1,24,20,384]{3,1,2,0:T(8,128)(2,1)} %param.6) | copy-start | bytes 1105924
  113.2 50.7 %copy-start.3 = (bf16[1,24,20,384]{3,1,2,0:T(8,128)(2,1)S(1)}, bf16[1,24,20,384]{3,1,2,0:T(8,128)(2,1)}, u32[]{:S(2)}) copy-start(bf16[1,24,20,384]{3,1,2,0:T(8,128)(2,1)} %param.10) | copy-start | bytes 1105924
  129.2 34.7 %collective-permute-start.2 = (bf16[4,4,112,384]{3,2,1,0:T(8,128)(2,1)S(1)}, bf16[4,4,112,384]{3,2,1,0:T(8,128)(2,1)S(1)}, u32[]{:S(2)}, u32[]{:S(2)}) collective-permute-start(bf16[4,4,112,384]{3,2,1,0:T(8,128)(2,1)S(1)} %all_to_all.16.held), channel_id=1, source_target_pairs={{0,128},{128,0},{1,129},{129,1},{2,130},{130,2},{3,131},{131,3},{4... | collective-permute-start | bytes 4128776 | tf_op jit(solution)/shard_map/ppermute | solution.py:261
  136.5 6.2 %collective-permute-start.3 = (f32[28,384]{1,0:T(8,128)S(1)}, f32[28,384]{1,0:T(8,128)S(1)}, u32[]{:S(2)}, u32[]{:S(2)}) collective-permute-start(f32[28,384]{1,0:T(8,128)S(1)} %convert_reduce_fusion), channel_id=1, source_target_pairs={{0,256},{256,0},{512,768},{768,512},{1,257},{257,1},{513,769},{769... | collective-permute-start | bytes 129032 | tf_op jit(solution)/shard_map/ppermute | solution.py:198
  142.7 8.8 %collective-permute-start.4 = (f32[28,384]{1,0:T(8,128)S(1)}, f32[28,384]{1,0:T(8,128)S(1)}, u32[]{:S(2)}, u32[]{:S(2)}) collective-permute-start(f32[28,384]{1,0:T(8,128)S(1)} %add.15), channel_id=1, source_target_pairs={{0,512},{256,768},{512,0},{768,256},{1,513},{257,769},{513,1},{769... | collective-permute-start | bytes 129032 | tf_op jit(solution)/shard_map/ppermute | solution.py:198
  151.5 9.2 %collective-permute-start.6 = (f32[28,384]{1,0:T(8,128)S(1)}, f32[28,384]{1,0:T(8,128)S(1)}, u32[]{:S(2)}, u32[]{:S(2)}) collective-permute-start(f32[28,384]{1,0:T(8,128)S(1)} %add.16), channel_id=1, source_target_pairs={{0,0},{8,128},{128,8},{136,136},{1,1},{9,129},{129,9},{137,137},{2... | collective-permute-start | bytes 129032 | tf_op jit(solution)/shard_map/ppermute | solution.py:200
  158.6 3.1 %collective-permute-start.5 = (f32[28,384]{1,0:T(8,128)S(1)}, f32[28,384]{1,0:T(8,128)S(1)}, u32[]{:S(2)}, u32[]{:S(2)}) collective-permute-start(f32[28,384]{1,0:T(8,128)S(1)} %add.16), channel_id=1, source_target_pairs={{8,0},{128,136},{136,8},{0,128},{9,1},{129,137},{137,9},{1,129},{1... | collective-permute-start | bytes 129032 | tf_op jit(solution)/shard_map/ppermute | solution.py:200
  163.9 1.0 copy-start.5
